TPU v7x, 32 devices: a whole 2x2x4 slice. The times are simulated.
32 devices in a mesh: batch: 16 (over z, x, core), head: 2 (over y).
Axes of the slice: x: 2, y: 2, z: 4, core: 2. Of those that a mesh axis runs over, the one named last changes fastest.
Arguments:
- clip_in: bfloat16 [16, 6272, 192], P('batch', 'head'), may hold values from -6 to 6
- frame_count: int32 [16], P('batch'), may hold values from 2 to 8, as said below
- frame_mask: int32 [16, 8], P('batch'), may hold values from 0 to 1, as said below
- pool_index: int32 [16, 1568], P('batch'), may hold values from 0 to 3
- first_norm_gain: float32 [192], replicated, may hold values from 0.25 to 1.75
- first_norm_bias: float32 [192], replicated, may hold values from -1.75 to 1.75
- first_widen_weight: bfloat16 [192, 384], replicated, may hold values from -0.4375 to 0.4375
- first_widen_bias: float32 [384], replicated, may hold values from -1.75 to 1.75
- first_qkv_weight: bfloat16 [192, 3, 384], P(None, None, 'head'), may hold values from -0.4375 to 0.4375
- first_qv_bias: float32 [2, 384], P(None, 'head'), may hold values from -1.75 to 1.75
- first_out_weight: bfloat16 [384, 384], P('head'), may hold values from -6 to 6
- first_out_bias: float32 [384], replicated, may hold values from -1.75 to 1.75
- first_mlp_gain: float32 [384], replicated, may hold values from 0.25 to 1.75
- first_mlp_bias: float32 [384], replicated, may hold values from -1.75 to 1.75
- first_up_weight: bfloat16 [384, 1536], P(None, 'head'), may hold values from -0.3125 to 0.3125
- first_up_bias: float32 [1536], P('head'), may hold values from -1.75 to 1.75
- first_down_weight: bfloat16 [1536, 384], P('head'), may hold values from -0.15625 to 0.15625
- first_down_bias: float32 [384], replicated, may hold values from -1.75 to 1.75
- second_norm_gain: float32 [384], replicated, may hold values from 0.25 to 1.75
- second_norm_bias: float32 [384], replicated, may hold values from -1.75 to 1.75
- second_qkv_weight: bfloat16 [384, 3, 384], P(None, None, 'head'), may hold values from -0.3125 to 0.3125
- second_qv_bias: float32 [2, 384], P(None, 'head'), may hold values from -1.75 to 1.75
- second_out_weight: bfloat16 [384, 384], P('head'), may hold values from -6 to 6
- second_out_bias: float32 [384], replicated, may hold values from -1.75 to 1.75
- second_mlp_gain: float32 [384], replicated, may hold values from 0.25 to 1.75
- second_mlp_bias: float32 [384], replicated, may hold values from -1.75 to 1.75
- second_up_weight: bfloat16 [384, 1536], P(None, 'head'), may hold values from -0.3125 to 0.3125
- second_up_bias: float32 [1536], P('head'), may hold values from -1.75 to 1.75
- second_down_weight: bfloat16 [1536, 384], P('head'), may hold values from -0.15625 to 0.15625
- second_down_bias: float32 [384], replicated, may hold values from -1.75 to 1.75
- cotangent: bfloat16 [16, 1568, 384], P('batch', 'head'), may hold values from -6 to 6
Outputs:
- layer_output: bfloat16 [16, 1568, 384], P('batch', 'head')
- input_gradient: float32 [16, 6272, 192], P('batch', 'head')
- grad_first_norm_gain: float32 [192], replicated
- grad_first_norm_bias: float32 [192], replicated
- grad_first_widen_weight: float32 [192, 384], replicated
- grad_first_widen_bias: float32 [384], replicated
- grad_first_qkv_weight: float32 [192, 3, 384], P(None, None, 'head')
- grad_first_qv_bias: float32 [2, 384], P(None, 'head')
- grad_first_out_weight: float32 [384, 384], P('head')
- grad_first_out_bias: float32 [384], replicated
- grad_first_mlp_gain: float32 [384], replicated
- grad_first_mlp_bias: float32 [384], replicated
- grad_first_up_weight: float32 [384, 1536], P(None, 'head')
- grad_first_up_bias: float32 [1536], P('head')
- grad_first_down_weight: float32 [1536, 384], P('head')
- grad_first_down_bias: float32 [384], replicated
- grad_second_norm_gain: float32 [384], replicated
- grad_second_norm_bias: float32 [384], replicated
- grad_second_qkv_weight: float32 [384, 3, 384], P(None, None, 'head')
- grad_second_qv_bias: float32 [2, 384], P(None, 'head')
- grad_second_out_weight: float32 [384, 384], P('head')
- grad_second_out_bias: float32 [384], replicated
- grad_second_mlp_gain: float32 [384], replicated
- grad_second_mlp_bias: float32 [384], replicated
- grad_second_up_weight: float32 [384, 1536], P(None, 'head')
- grad_second_up_bias: float32 [1536], P('head')
- grad_second_down_weight: float32 [1536, 384], P('head')
- grad_second_down_bias: float32 [384], replicated
Inputs may be any that keep to these rules, and one draw needn't show every extreme that they name: `frame_count`: at least one clip has all 8 frames. `frame_mask`: frame 0 of every clip is marked 1, and so is every frame of some clip that has all 8 frames.
All inputs are finite; a program needn't handle non-finite values.
Results may differ from a plain program's by a relative error of at most 0.013.
Values may be sent and summed in bfloat16 or wider, within the bound.
No kernel may reach another device: no remote copies, remote signals or barrier semaphores. Data moves between devices by JAX's collectives and lax.ppermute only.
A program may use at most 256 MiB of HBM per device.

v0:
```python
import jax
import jax.numpy as jnp
from jax import lax
from jax.sharding import PartitionSpec as P

HEAD_DIM = 96
SIDE = 14
QBLOCK = 784


eps_norm = 1e-06


def layer_norm(residual, norm_gain, norm_shift):
    centered = residual - jnp.mean(residual, axis=-1, keepdims=True)
    spread = jnp.mean(centered * centered, axis=-1, keepdims=True)
    return centered * lax.rsqrt(spread + eps_norm) * norm_gain + norm_shift


def window_weights(pool_picks):
    leading = pool_picks.shape[:-1]
    frames = pool_picks.shape[-1] // (SIDE * SIDE)
    onehot = (pool_picks[..., None] == jnp.arange(4, dtype=jnp.int32)).astype(jnp.float32)
    onehot = onehot.reshape(leading + (frames, SIDE, SIDE, 2, 2))
    return jnp.swapaxes(onehot, -3, -2)[..., None]


def pool_rows(tensor, onehot):
    leading = onehot.shape[:-6]
    frames = onehot.shape[-6]
    features = tensor.shape[-1]
    blocks = tensor.reshape(leading + (frames, SIDE, 2, SIDE, 2, features))
    return jnp.sum(blocks * onehot, axis=(-4, -2)).reshape(
        leading + (frames * SIDE * SIDE, features)
    )


def unpool_rows(tensor, onehot):
    leading = onehot.shape[:-6]
    frames = onehot.shape[-6]
    features = tensor.shape[-1]
    blocks = tensor.reshape(leading + (frames, SIDE, 1, SIDE, 1, features))
    return (blocks * onehot.astype(tensor.dtype)).reshape(
        leading + (frames * 4 * SIDE * SIDE, features)
    )


def attend_clip(pieces):
    query_rows, key_rows, value_rows, live_keys = pieces
    heads_local = query_rows.shape[1] // HEAD_DIM
    number_blocks = query_rows.shape[0] // QBLOCK
    scaling = HEAD_DIM ** (-0.5)

    def one_block(query_block):
        outputs, totals = ([], [])
        for head_index in range(heads_local):
            columns = slice(head_index * HEAD_DIM, (head_index + 1) * HEAD_DIM)
            scores = (
                jnp.einsum(
                    "qd,kd->qk",
                    query_block[:, columns],
                    key_rows[:, columns],
                    preferred_element_type=jnp.float32,
                )
                * scaling
            )
            scores = jnp.where(live_keys[None, :], scores, -1e30)
            row_peak = jnp.max(scores, axis=1, keepdims=True)
            weights = jnp.exp(scores - row_peak)
            row_total = jnp.sum(weights, axis=1, keepdims=True)
            softmaxed = (weights / row_total).astype(jnp.bfloat16)
            outputs.append(
                jnp.dot(softmaxed, value_rows[:, columns], preferred_element_type=jnp.float32)
            )
            totals.append(row_peak[:, 0] + jnp.log(row_total[:, 0]))
        return (jnp.concatenate(outputs, axis=1).astype(jnp.bfloat16), jnp.stack(totals))

    blocks = query_rows.reshape(number_blocks, QBLOCK, query_rows.shape[1])
    attended, totals = lax.map(one_block, blocks)
    return (attended.reshape(query_rows.shape), totals)


def attend_back(pieces):
    query_rows, key_rows, value_rows, live_keys, totals, grad_attended = pieces
    heads_local = query_rows.shape[1] // HEAD_DIM
    number_blocks = query_rows.shape[0] // QBLOCK
    scaling = HEAD_DIM ** (-0.5)

    def one_block(carried, block_pieces):
        key_grad, value_grad = carried
        query_block, total_block, grad_block = block_pieces
        query_parts, key_parts, value_parts = ([], [], [])
        for head_index in range(heads_local):
            columns = slice(head_index * HEAD_DIM, (head_index + 1) * HEAD_DIM)
            key_head = key_rows[:, columns]
            value_head = value_rows[:, columns]
            query_head = query_block[:, columns]
            grad_head = grad_block[:, columns]
            scores = (
                jnp.einsum("qd,kd->qk", query_head, key_head, preferred_element_type=jnp.float32)
                * scaling
            )
            scores = jnp.where(live_keys[None, :], scores, -1e30)
            softmaxed = jnp.exp(scores - total_block[head_index][:, None])
            prob_grads = jnp.einsum(
                "qd,kd->qk", grad_head, value_head, preferred_element_type=jnp.float32
            )
            row_inner = jnp.sum(softmaxed * prob_grads, axis=1, keepdims=True)
            score_grads = (softmaxed * (prob_grads - row_inner)).astype(jnp.bfloat16)
            query_parts.append(
                jnp.dot(score_grads, key_head, preferred_element_type=jnp.float32) * scaling
            )
            key_parts.append(
                jnp.einsum("qk,qd->kd", score_grads, query_head, preferred_element_type=jnp.float32)
                * scaling
            )
            value_parts.append(
                jnp.einsum(
                    "qk,qd->kd",
                    softmaxed.astype(jnp.bfloat16),
                    grad_head,
                    preferred_element_type=jnp.float32,
                )
            )
        key_grad = key_grad + jnp.concatenate(key_parts, axis=1)
        value_grad = value_grad + jnp.concatenate(value_parts, axis=1)
        return ((key_grad, value_grad), jnp.concatenate(query_parts, axis=1))

    zeros_keys = jnp.zeros(key_rows.shape, jnp.float32)
    block_inputs = (
        query_rows.reshape(number_blocks, QBLOCK, query_rows.shape[1]),
        totals,
        grad_attended.reshape(number_blocks, QBLOCK, query_rows.shape[1]),
    )
    (key_grad, value_grad), query_grad = lax.scan(one_block, (zeros_keys, zeros_keys), block_inputs)
    return (query_grad.reshape(query_rows.shape), key_grad, value_grad)


def rows_gather(own_rows):
    return lax.all_gather(own_rows, "head", axis=1, tiled=True)


def rows_reduce(partial_rows):
    return lax.psum_scatter(partial_rows, "head", scatter_dimension=1, tiled=True)


def layer_forward(residual, params, frame_live, pick_all, pick_own):
    (
        norm_gain,
        norm_shift,
        widen_weight,
        widen_bias,
        qkv_weight,
        qv_bias,
        out_weight,
        out_bias,
        mlp_gain,
        mlp_shift,
        up_weight,
        up_bias,
        down_weight,
        down_bias,
    ) = params
    own_low = layer_norm(residual, norm_gain, norm_shift).astype(jnp.bfloat16)
    gathered = rows_gather(own_low)
    projected = jnp.einsum(
        "btc,cjd->btjd", gathered, qkv_weight, preferred_element_type=jnp.float32
    )
    query_rows = projected[:, :, 0] + qv_bias[0]
    if pick_all is not None:
        query_rows = pool_rows(query_rows, pick_all)
    query_rows = query_rows.astype(jnp.bfloat16)
    key_rows = projected[:, :, 1].astype(jnp.bfloat16)
    value_rows = (projected[:, :, 2] + qv_bias[1]).astype(jnp.bfloat16)
    live_keys = jnp.repeat(frame_live, key_rows.shape[1] // frame_live.shape[1], axis=1)
    attended, totals = lax.map(attend_clip, (query_rows, key_rows, value_rows, live_keys))
    partial_branch = jnp.einsum(
        "btd,de->bte", attended, out_weight, preferred_element_type=jnp.float32
    )
    branch = lax.psum_scatter(partial_branch, "head", scatter_dimension=1, tiled=True)
    branch = branch + out_bias
    if widen_weight is not None:
        widened = (
            jnp.einsum("btc,ce->bte", own_low, widen_weight, preferred_element_type=jnp.float32)
            + widen_bias
        )
        middle = pool_rows(widened, pick_own) + branch
    else:
        middle = residual + branch
    gathered_mid = rows_gather(layer_norm(middle, mlp_gain, mlp_shift).astype(jnp.bfloat16))
    hidden = (
        jnp.einsum("btc,cf->btf", gathered_mid, up_weight, preferred_element_type=jnp.float32)
        + up_bias
    )
    active = jax.nn.gelu(hidden, approximate=False).astype(jnp.bfloat16)
    partial_feed = jnp.einsum(
        "btf,fc->btc", active, down_weight, preferred_element_type=jnp.float32
    )
    feed = lax.psum_scatter(partial_feed, "head", scatter_dimension=1, tiled=True)
    output = middle + feed + down_bias
    kept = (
        residual,
        own_low,
        gathered,
        query_rows,
        key_rows,
        value_rows,
        live_keys,
        attended,
        totals,
        None,
        middle,
        gathered_mid,
        hidden,
    )
    return (output, kept)


def layer_backward(grad_output, kept, params, pick_all, pick_own):
    (
        norm_gain,
        norm_shift,
        widen_weight,
        widen_bias,
        qkv_weight,
        qv_bias,
        out_weight,
        out_bias,
        mlp_gain,
        mlp_shift,
        up_weight,
        up_bias,
        down_weight,
        down_bias,
    ) = params
    (
        residual,
        own_low,
        gathered,
        query_rows,
        key_rows,
        value_rows,
        live_keys,
        attended,
        totals,
        regrouped,
        middle,
        gathered_mid,
        hidden,
    ) = kept
    grad_rows = lax.all_gather(grad_output.astype(jnp.bfloat16), "head", axis=1, tiled=True)
    active = jax.nn.gelu(hidden, approximate=False).astype(jnp.bfloat16)
    grad_down = jnp.einsum("btf,btc->fc", active, grad_rows, preferred_element_type=jnp.float32)
    grad_down_bias = jnp.sum(grad_output, axis=(0, 1))
    grad_active = jnp.einsum(
        "btc,fc->btf", grad_rows, down_weight, preferred_element_type=jnp.float32
    )
    gelu_pull = jax.vjp(lambda inputs: jax.nn.gelu(inputs, approximate=False), hidden)[1]
    grad_hidden = gelu_pull(grad_active)[0].astype(jnp.bfloat16)
    grad_up = jnp.einsum(
        "btc,btf->cf", gathered_mid, grad_hidden, preferred_element_type=jnp.float32
    )
    grad_up_bias = jnp.sum(grad_hidden.astype(jnp.float32), axis=(0, 1))
    grad_normed_mid = rows_reduce(
        jnp.einsum("btf,cf->btc", grad_hidden, up_weight, preferred_element_type=jnp.float32)
    )
    norm_pull = jax.vjp(layer_norm, middle, mlp_gain, mlp_shift)[1]
    grad_middle, grad_mlp_gain, grad_mlp_shift = norm_pull(grad_normed_mid)
    grad_middle = grad_middle + grad_output
    grad_low = grad_middle.astype(jnp.bfloat16)
    grad_branch = lax.all_gather(grad_low, "head", axis=1, tiled=True)
    grad_out = jnp.einsum("btd,bte->de", attended, grad_branch, preferred_element_type=jnp.float32)
    grad_attended = jnp.einsum(
        "bte,de->btd", grad_branch, out_weight, preferred_element_type=jnp.float32
    ).astype(jnp.bfloat16)
    grad_out_bias = jnp.sum(grad_middle, axis=(0, 1))
    grad_query, grad_key, grad_value = lax.map(
        attend_back, (query_rows, key_rows, value_rows, live_keys, totals, grad_attended)
    )
    grad_query = grad_query.astype(jnp.bfloat16)
    grad_key = grad_key.astype(jnp.bfloat16)
    grad_value = grad_value.astype(jnp.bfloat16)
    grad_qv_bias = jnp.stack(
        [
            jnp.sum(grad_query.astype(jnp.float32), axis=(0, 1)),
            jnp.sum(grad_value.astype(jnp.float32), axis=(0, 1)),
        ]
    )
    if pick_all is not None:
        grad_query = unpool_rows(grad_query, pick_all)
    grad_projected = jnp.stack([grad_query, grad_key, grad_value], axis=2)
    grad_qkv = jnp.einsum(
        "btc,btjd->cjd", gathered, grad_projected, preferred_element_type=jnp.float32
    )
    grad_normed = rows_reduce(
        jnp.einsum("btjd,cjd->btc", grad_projected, qkv_weight, preferred_element_type=jnp.float32)
    )
    if widen_weight is not None:
        grad_widened = unpool_rows(grad_middle, pick_own).astype(jnp.bfloat16)
        grad_widen_bias = jnp.sum(grad_middle, axis=(0, 1))
        grad_widen = jnp.einsum(
            "btc,bte->ce", own_low, grad_widened, preferred_element_type=jnp.float32
        )
        grad_normed = grad_normed + jnp.einsum(
            "bte,ce->btc", grad_widened, widen_weight, preferred_element_type=jnp.float32
        )
    norm_pull = jax.vjp(layer_norm, residual, norm_gain, norm_shift)[1]
    grad_residual, grad_norm_gain, grad_norm_shift = norm_pull(grad_normed)
    split_parts = (grad_qkv, grad_qv_bias, grad_out, grad_up, grad_up_bias, grad_down)
    if widen_weight is not None:
        shared_parts = (
            grad_norm_gain,
            grad_norm_shift,
            grad_widen,
            grad_widen_bias,
            grad_out_bias,
            grad_mlp_gain,
            grad_mlp_shift,
            grad_down_bias,
        )
    else:
        grad_residual = grad_residual + grad_middle
        shared_parts = (
            grad_norm_gain,
            grad_norm_shift,
            grad_out_bias,
            grad_mlp_gain,
            grad_mlp_shift,
            grad_down_bias,
        )
    return (grad_residual, split_parts, shared_parts)


def shards(
    clip_in,
    frame_count,
    frame_mask,
    pool_index,
    first_norm_gain,
    first_norm_bias,
    first_widen_weight,
    first_widen_bias,
    first_qkv_weight,
    first_qv_bias,
    first_out_weight,
    first_out_bias,
    first_mlp_gain,
    first_mlp_bias,
    first_up_weight,
    first_up_bias,
    first_down_weight,
    first_down_bias,
    second_norm_gain,
    second_norm_bias,
    second_qkv_weight,
    second_qv_bias,
    second_out_weight,
    second_out_bias,
    second_mlp_gain,
    second_mlp_bias,
    second_up_weight,
    second_up_bias,
    second_down_weight,
    second_down_bias,
    cotangent,
):
    first = (
        first_norm_gain,
        first_norm_bias,
        first_widen_weight,
        first_widen_bias,
        first_qkv_weight,
        first_qv_bias,
        first_out_weight,
        first_out_bias,
        first_mlp_gain,
        first_mlp_bias,
        first_up_weight,
        first_up_bias,
        first_down_weight,
        first_down_bias,
    )
    second = (
        second_norm_gain,
        second_norm_bias,
        None,
        None,
        second_qkv_weight,
        second_qv_bias,
        second_out_weight,
        second_out_bias,
        second_mlp_gain,
        second_mlp_bias,
        second_up_weight,
        second_up_bias,
        second_down_weight,
        second_down_bias,
    )
    frame_live = (
        jnp.arange(frame_mask.shape[1], dtype=jnp.int32)[None, :] < frame_count[:, None]
    ) & (frame_mask == 1)
    own_pooled = clip_in.shape[1] // 4
    own_index = lax.dynamic_slice_in_dim(
        pool_index, lax.axis_index("head") * own_pooled, own_pooled, 1
    )
    pick_all = window_weights(pool_index)
    pick_own = window_weights(own_index)
    middle, kept_first = layer_forward(
        clip_in.astype(jnp.float32), first, frame_live, pick_all, pick_own
    )
    output, kept_second = layer_forward(middle, second, frame_live, None, None)
    grad_middle, split_second, shared_second = layer_backward(
        cotangent.astype(jnp.float32), kept_second, second, None, None
    )
    grad_input, split_first, shared_first = layer_backward(
        grad_middle, kept_first, first, pick_all, pick_own
    )
    summed = lax.psum(
        (
            split_first[0],
            split_first[1],
            split_first[2],
            split_first[3],
            split_first[4],
            split_first[5],
            split_second[0],
            split_second[1],
            split_second[2],
            split_second[3],
            split_second[4],
            split_second[5],
        ),
        "batch",
    )
    split_first = summed[:6]
    split_second = summed[6:]
    shared = lax.psum(
        (
            shared_first[0],
            shared_first[1],
            shared_first[2],
            shared_first[3],
            shared_first[4],
            shared_first[5],
            shared_first[6],
            shared_first[7],
            shared_second[0],
            shared_second[1],
            shared_second[2],
            shared_second[3],
            shared_second[4],
            shared_second[5],
        ),
        ("batch", "head"),
    )
    return (
        output.astype(jnp.bfloat16),
        grad_input,
        shared[0],
        shared[1],
        shared[2],
        shared[3],
        split_first[0],
        split_first[1],
        split_first[2],
        shared[4],
        shared[5],
        shared[6],
        split_first[3],
        split_first[4],
        split_first[5],
        shared[7],
        shared[8],
        shared[9],
        split_second[0],
        split_second[1],
        split_second[2],
        shared[10],
        shared[11],
        shared[12],
        split_second[3],
        split_second[4],
        split_second[5],
        shared[13],
    )


def solution(mesh):
    in_specs = (
        P("batch", "head", None),
        P("batch"),
        P("batch", None),
        P("batch", None),
        P(),
        P(),
        P(),
        P(),
        P(None, None, "head"),
        P(None, "head"),
        P("head", None),
        P(),
        P(),
        P(),
        P(None, "head"),
        P("head"),
        P("head", None),
        P(),
        P(),
        P(),
        P(None, None, "head"),
        P(None, "head"),
        P("head", None),
        P(),
        P(),
        P(),
        P(None, "head"),
        P("head"),
        P("head", None),
        P(),
        P("batch", "head", None),
    )
    out_specs = (
        P("batch", "head", None),
        P("batch", "head", None),
        P(),
        P(),
        P(),
        P(),
        P(None, None, "head"),
        P(None, "head"),
        P("head", None),
        P(),
        P(),
        P(),
        P(None, "head"),
        P("head"),
        P("head", None),
        P(),
        P(),
        P(),
        P(None, None, "head"),
        P(None, "head"),
        P("head", None),
        P(),
        P(),
        P(),
        P(None, "head"),
        P("head"),
        P("head", None),
        P(),
    )
    return jax.shard_map(shards, mesh=mesh, in_specs=in_specs, out_specs=out_specs, check_vma=False)
```

profile of v0, /device:TPU:0, one launch (start us, length us, event | category | flops | bytes accessed | tf_op | source)
XLA Modules:
  0.0 1541.9 jit_solution(13023392979771071150)
XLA Ops:
  21.6 81.7 %all-gather.9.cloned.1.call-done = bf16[1,6272,192]{2,0,1:T(2,128)(2,1)} async-done(((bf16[1,3136,192]{2,0,1:T(2,128)(2,1)}), bf16[1,6272,192]{2,0,1:T(2,128)(2,1)}) %all-gather.9.cloned.1.call-update) | async-done | bytes 2408464 | tf_op jit(solution)/shard_map/all_gather | solution.py:140
  103.3 14.1 copy.91
  131.6 14.2 copy.93
  145.8 13.7 multiply_reduce_fusion.4
  160.9 125.7 %while.96 = (s32[]{:T(128)}, bf16[2,784,192]{1,2,0:T(8,128)(2,1)S(1)}, f32[2,2,784]{2,1,0:T(2,128)S(1)}, bf16[2,784,192]{2,1,0:T(8,128)(2,1)}, bf16[6272,192]{1,...) while((s32[]{:T(128)}, ...), condition=%wide.region_9.10_spmd.clone, body=%wide.region_4.9_spmd.clone.sunk | while | flops 3895213056 | bytes 145829744 | solution.py:79
  162.4 11.8 fusion.300
  174.2 18.8 %fusion.301 = (f32[784]{0:T(1024)S(1)}, f32[784]{0:T(1024)S(1)}, f32[784,6272]{1,0:T(8,128)}) fusion(f32[784,6272]{1,0:T(8,128)} %get-tuple-element.922, f32[784]{0:T(1024)S(1)} %get-tuple-element.923, pred[6272]{0:T(1024)(128)(4,1)S(1)} %broadcast_in_dim.393, bf16[6272,192]{1,0:T(8,128)(2,1)S(1)} %copy-done.6, ...), kind=kOutput, calls=%fused_computation.12.clone.1 | convolution fusion | flops 978530816 | bytes 41161856 | tf_op jit(solution)/shard_map/while/body/eval_jaxpr/while/body/eval_jaxpr/qd,kd->qk/dot_general | solution.py:59
  193.0 9.3 fusion.304
  202.3 11.0 fusion.302
  213.3 10.3 fusion.303
  224.9 11.8 fusion.300
  236.7 18.8 %fusion.301 = (f32[784]{0:T(1024)S(1)}, f32[784]{0:T(1024)S(1)}, f32[784,6272]{1,0:T(8,128)}) fusion(f32[784,6272]{1,0:T(8,128)} %get-tuple-element.922, f32[784]{0:T(1024)S(1)} %get-tuple-element.923, pred[6272]{0:T(1024)(128)(4,1)S(1)} %broadcast_in_dim.393, bf16[6272,192]{1,0:T(8,128)(2,1)S(1)} %copy-done.6, ...), kind=kOutput, calls=%fused_computation.12.clone.1 | convolution fusion | flops 978530816 | bytes 41161856 | tf_op jit(solution)/shard_map/while/body/eval_jaxpr/while/body/eval_jaxpr/qd,kd->qk/dot_general | solution.py:59
  255.5 9.3 fusion.304
  264.8 11.0 fusion.302
  275.8 10.3 fusion.303
  294.1 7.2 reshape.1142
  309.6 16.3 %reduce-scatter.11.cloned.1.call-done = f32[1,784,384]{2,1,0:T(8,128)} async-done(((f32[1,1568,384]{2,1,0:T(8,128)}), f32[1,784,384]{2,1,0:T(8,128)}) %reduce-scatter.11.cloned.1.call-update) | async-done | bytes 1204240 | tf_op jit(solution)/shard_map/reduce_scatter | solution.py:180
  329.1 23.1 %all-gather.11.cloned.1.call-done = bf16[1,1568,384]{2,1,0:T(8,128)(2,1)} async-done(((bf16[1,784,384]{2,1,0:T(8,128)(2,1)}), bf16[1,1568,384]{2,1,0:T(8,128)(2,1)}) %all-gather.11.cloned.1.call-update) | async-done | bytes 1204240 | tf_op jit(solution)/shard_map/all_gather | solution.py:140
  352.2 13.9 multiply_convert_fusion.7
  370.7 35.2 %reduce-scatter.13.cloned.1.call-done = f32[1,784,384]{2,1,0:T(8,128)} async-done(((f32[1,1568,384]{2,1,0:T(8,128)}), f32[1,784,384]{2,1,0:T(8,128)}) %reduce-scatter.13.cloned.1.call-update) | async-done | bytes 1204240 | tf_op jit(solution)/shard_map/reduce_scatter | solution.py:199
  409.0 23.1 %all-gather.13.cloned.1.call-done = bf16[1,1568,384]{2,1,0:T(8,128)(2,1)} async-done(((bf16[1,784,384]{2,1,0:T(8,128)(2,1)}), bf16[1,1568,384]{2,1,0:T(8,128)(2,1)}) %all-gather.13.cloned.1.call-update) | async-done | bytes 1204240 | tf_op jit(solution)/shard_map/all_gather | solution.py:140
  445.7 20.4 %while.97 = (s32[]{:T(128)}, bf16[2,784,192]{1,2,0:T(8,128)(2,1)}, f32[2,2,784]{2,1,0:T(2,128)S(1)}, bf16[2,784,192]{2,1,0:T(8,128)(2,1)}, bf16[1568,192]{1,0:T(...) while((s32[]{:T(128)}, bf16[2,784,192]{1,2,0:T(8,128)(2,1)}, ...), condition=%wide.region_21.22_spmd.clone, body=%wide.region_16.21_spmd.clone.sunk | while | flops 974367744 | bytes 41326852 | solution.py:79
  474.8 35.3 %reduce-scatter.15.cloned.1.call-done = f32[1,784,384]{2,1,0:T(8,128)} async-done(((f32[1,1568,384]{2,1,0:T(8,128)}), f32[1,784,384]{2,1,0:T(8,128)}) %reduce-scatter.15.cloned.1.call-update) | async-done | bytes 1204240 | tf_op jit(solution)/shard_map/reduce_scatter | solution.py:180
  514.7 22.4 %all-gather.15.cloned.1.call-done = bf16[1,1568,384]{2,1,0:T(8,128)(2,1)} async-done(((bf16[1,784,384]{2,1,0:T(8,128)(2,1)}), bf16[1,1568,384]{2,1,0:T(8,128)(2,1)}) %all-gather.15.cloned.1.call-update) | async-done | bytes 1204240 | tf_op jit(solution)/shard_map/all_gather | solution.py:140
  537.1 14.3 multiply_convert_fusion.6
  551.4 10.4 all-gather.17.cloned.1.call-done
  561.8 6.8 convert_reduce_fusion
  577.8 30.6 %reduce-scatter.19.cloned.1.call-done = f32[1,784,384]{2,1,0:T(8,128)} async-done(((f32[1,1568,384]{2,1,0:T(8,128)}), f32[1,784,384]{2,1,0:T(8,128)}) %reduce-scatter.19.cloned.1.call-update) | async-done | bytes 1204240 | tf_op jit(solution)/shard_map/reduce_scatter | solution.py:144
  610.8 35.0 %reduce-scatter.17.cloned.1.call-done = f32[1,784,384]{2,1,0:T(8,128)} async-done(((f32[1,1568,384]{2,1,0:T(8,128)}), f32[1,784,384]{2,1,0:T(8,128)}) %reduce-scatter.17.cloned.1.call-update) | async-done | bytes 1204240 | tf_op jit(solution)/shard_map/reduce_scatter | solution.py:199
  652.1 23.1 %all-gather.19.cloned.1.call-done = bf16[1,1568,384]{2,1,0:T(8,128)(2,1)} async-done(((bf16[1,784,384]{2,1,0:T(8,128)(2,1)}), bf16[1,1568,384]{2,1,0:T(8,128)(2,1)}) %all-gather.19.cloned.1.call-update) | async-done | bytes 1204240 | tf_op jit(solution)/shard_map/all_gather | solution.py:271
  681.2 36.1 %while.98 = (s32[]{:T(128)}, f32[1568,192]{0,1:T(8,128)}, f32[1568,192]{0,1:T(8,128)S(1)}, bf16[2,784,192]{1,2,0:T(8,128)(2,1)}, bf16[2,784,192]{2,1,0:T(8,128)(...) while((s32[]{:T(128)}, f32[1568,192]{0,1:T(8,128)}, ...), condition=%wide.region_32.33_spmd.clone, body=%wide.region_29.32_spmd.clone.sunk | while | flops 2385415680 | bytes 105899400 | solution.py:135
  727.5 35.3 %reduce-scatter.21.cloned.1.call-done = f32[1,784,384]{2,1,0:T(8,128)} async-done(((f32[1,1568,384]{2,1,0:T(8,128)}), f32[1,784,384]{2,1,0:T(8,128)}) %reduce-scatter.21.cloned.1.call-update) | async-done | bytes 1204240 | tf_op jit(solution)/shard_map/reduce_scatter | solution.py:144
  770.0 23.2 %all-gather.21.cloned.1.call-done = bf16[1,1568,384]{2,1,0:T(8,128)(2,1)} async-done(((bf16[1,784,384]{2,1,0:T(8,128)(2,1)}), bf16[1,1568,384]{2,1,0:T(8,128)(2,1)}) %all-gather.21.cloned.1.call-update) | async-done | bytes 1204240 | tf_op jit(solution)/shard_map/all_gather | solution.py:251
  793.2 6.8 convert_reduce_fusion.1
  804.4 35.3 %reduce-scatter.23.cloned.1.call-done = f32[1,784,384]{2,1,0:T(8,128)} async-done(((f32[1,1568,384]{2,1,0:T(8,128)}), f32[1,784,384]{2,1,0:T(8,128)}) %reduce-scatter.23.cloned.1.call-update) | async-done | bytes 1204240 | tf_op jit(solution)/shard_map/reduce_scatter | solution.py:144
  847.0 21.9 %all-gather.23.cloned.1.call-done = bf16[1,1568,384]{2,1,0:T(8,128)(2,1)} async-done(((bf16[1,784,384]{2,1,0:T(8,128)(2,1)}), bf16[1,1568,384]{2,1,0:T(8,128)(2,1)}) %all-gather.23.cloned.1.call-update) | async-done | bytes 1204240 | tf_op jit(solution)/shard_map/all_gather | solution.py:271
  872.8 251.2 %while.99 = (s32[]{:T(128)}, f32[6272,192]{0,1:T(8,128)}, f32[6272,192]{0,1:T(8,128)}, bf16[2,784,192]{1,2,0:T(8,128)(2,1)}, bf16[2,784,192]{2,1,0:T(8,128)(2,1)...) while((s32[]{:T(128)}, f32[6272,192]{0,1:T(8,128)}, ...), condition=%wide.region_42.43_spmd.clone, body=%wide.region_39.42_spmd.clone.sunk | while | flops 9538958336 | bytes 636083456 | solution.py:135
  875.5 9.7 fusion.352
  885.2 8.2 fusion.351
  893.4 14.3 multiply_reduce_fusion.21
  907.7 17.2 %multiply_convert_fusion.15 = bf16[784,6272]{1,0:T(8,128)(2,1)} fusion(f32[784,6272]{1,0:T(8,128)} %get-tuple-element.972, f32[784,6272]{1,0:T(8,128)} %fusion.351, f32[784]{0:T(1024)S(1)} %get-tuple-element.973), kind=kLoop, calls=%fused_computation.110.clone.1 | loop fusion | flops 14751744 | bytes 49175616 | tf_op jit(solution)/shard_map/while/body/eval_jaxpr/while/body/eval_jaxpr/convert_element_type | solution.py:109
  932.6 7.3 fusion.355
  943.4 13.6 multiply_reduce_fusion.22
  957.0 17.2 %multiply_convert_fusion.16 = bf16[784,6272]{1,0:T(8,128)(2,1)} fusion(f32[784,6272]{1,0:T(8,128)} %get-tuple-element.975, f32[784,6272]{1,0:T(8,128)} %fusion.352, f32[784]{0:T(1024)S(1)} %get-tuple-element.976), kind=kLoop, calls=%fused_computation.113.clone.1 | loop fusion | flops 14751744 | bytes 49175616 | tf_op jit(solution)/shard_map/while/body/eval_jaxpr/while/body/eval_jaxpr/convert_element_type | solution.py:109
  981.9 7.1 fusion.356
  999.6 9.7 fusion.352
  1009.3 8.2 fusion.351
  1017.5 14.3 multiply_reduce_fusion.21
  1031.7 17.2 %multiply_convert_fusion.15 = bf16[784,6272]{1,0:T(8,128)(2,1)} fusion(f32[784,6272]{1,0:T(8,128)} %get-tuple-element.972, f32[784,6272]{1,0:T(8,128)} %fusion.351, f32[784]{0:T(1024)S(1)} %get-tuple-element.973), kind=kLoop, calls=%fused_computation.110.clone.1 | loop fusion | flops 14751744 | bytes 49175616 | tf_op jit(solution)/shard_map/while/body/eval_jaxpr/while/body/eval_jaxpr/convert_element_type | solution.py:109
  1056.7 7.3 fusion.355
  1067.5 13.6 multiply_reduce_fusion.22
  1081.1 17.2 %multiply_convert_fusion.16 = bf16[784,6272]{1,0:T(8,128)(2,1)} fusion(f32[784,6272]{1,0:T(8,128)} %get-tuple-element.975, f32[784,6272]{1,0:T(8,128)} %fusion.352, f32[784]{0:T(1024)S(1)} %get-tuple-element.976), kind=kLoop, calls=%fused_computation.113.clone.1 | loop fusion | flops 14751744 | bytes 49175616 | tf_op jit(solution)/shard_map/while/body/eval_jaxpr/while/body/eval_jaxpr/convert_element_type | solution.py:109
  1105.9 7.1 fusion.356
  1116.2 6.8 maximum_add_fusion.7
  1132.2 7.6 mul.564
  1176.9 6.3 convert_element_type.309
  1186.8 6.8 fusion.131
  1199.5 7.2 mul.569
  1206.9 61.2 %all-reduce.1 = (f32[2,192]{1,0:T(2,128)}, f32[768]{0:T(1024)}, f32[2,192]{1,0:T(2,128)}, f32[768]{0:T(1024)}) all-reduce(f32[2,192]{1,0:T(2,128)S(1)} %pad_maximum_fusion.1, f32[768]{0:T(1024)S(1)} %copy-done.127, f32[2,192]{1,0:T(2,128)S(1)} %pad_maximum_fusion.2, ...), channel_id=1, replica_groups=mesh['batch'=16,'head'=2] {'batch'}, use_global_device_ids=true, to_apply=%region_56.57 | all-reduce | flops 2304 | bytes 18432 | tf_op jit(solution)/shard_map/psum | solution.py:418
  1268.0 9.1 reshape_bitcast_fusion
  1277.2 7.7 copy.114
  1292.2 37.6 %all-reduce = (f32[192]{0:T(256)}, f32[192]{0:T(256)}, f32[384]{0:T(512)S(1)}, f32[384]{0:T(512)}, f32[384]{0:T(512)}, /*index=5*/f32[384]{0:T(512)}, f32[384]{0...) all-reduce(f32[192]{0:T(256)S(1)} %get-tuple-element.540, ...), channel_id=1, replica_groups=mesh['batch'=16,'head'=2] {'batch','head'}, use_global_device_ids=true, to_apply=%region_47.48 | all-reduce | flops 4224 | bytes 33792 | tf_op jit(solution)/shard_map/psum | solution.py:437
  1333.5 31.9 %all-reduce.6.cloned.1.call-done = f32[192,384]{1,0:T(8,128)} async-done(((f32[192,384]{1,0:T(8,128)}), f32[192,384]{1,0:T(8,128)}) %all-reduce.6.cloned.1.call-update) | async-done | bytes 294928 | tf_op jit(solution)/shard_map/psum | solution.py:437
  1365.4 157.6 %all-reduce.8.cloned.1.call-done = (f32[192,3,192]{2,0,1:T(8,128)}, f32[192,384]{1,0:T(8,128)}, f32[384,768]{1,0:T(8,128)}, f32[768,384]{1,0:T(8,128)}, f32[384,...) async-done(((f32[192,3,192]{2,0,1:T(8,128)}, f32[192,384]{1,0:T(8,128)}, f32[384,768]{1,0:T(8,128)}, f32[768,384]{1,0:T(8,128)}, ...) | async-done | bytes 6635536 | tf_op jit(solution)/shard_map/psum | solution.py:418
  (629 shorter events, 328.6 us)
Async XLA Ops:
  7.2 529.9 %copy-start = (bf16[384,768]{1,0:T(8,128)(2,1)S(1)}, bf16[384,768]{1,0:T(8,128)(2,1)}, u32[]{:S(2)}) copy-start(bf16[384,768]{1,0:T(8,128)(2,1)} %param.65) | copy-start | bytes 1769476
  7.2 96.1 %all-gather.9.cloned.1.call-start = ((), (), s32[]{:S(2)}) async-start(), calls=%async_computation.8 | async-start | bytes 9633792 | tf_op jit(solution)/shard_map/all_gather | solution.py:140
  18.6 307.4 %reduce-scatter.11.cloned.1.call-start = ((), (), s32[]{:S(2)}) async-start(), calls=%async_computation.9 | async-start | bytes 3612672 | tf_op jit(solution)/shard_map/reduce_scatter | solution.py:180
  19.6 97.8 %copy-start.123 = (s32[2,2]{1,0:T(2,128)}, s32[2,2]{1,0:T(2,128)S(1)}, u32[]{:S(2)}) copy-start(s32[2,2]{1,0:T(2,128)S(1)} %multiply_add_fusion.4) | copy-start | bytes 52
  160.9 127.5 %copy-start.74 = (bf16[192,384]{1,0:T(8,128)(2,1)S(1)}, bf16[192,384]{1,0:T(8,128)(2,1)}, u32[]{:S(2)}) copy-start(bf16[192,384]{1,0:T(8,128)(2,1)} %param.49) | copy-start | bytes 442372
  290.5 61.7 %all-gather.11.cloned.1.call-start = ((), (), s32[]{:S(2)}) async-start(), calls=%async_computation.10 | async-start | bytes 1806336 | tf_op jit(solution)/shard_map/all_gather | solution.py:140
  309.6 42.6 %copy-start.148 = (f32[768]{0:T(1024)S(1)}, f32[768]{0:T(1024)}, u32[]{:S(2)}) copy-start(f32[768]{0:T(1024)} %param.54) | copy-start | bytes 9220
  327.5 78.4 %copy-start.17 = (f32[1,784,384]{2,1,0:T(8,128)}, f32[1,784,384]{2,1,0:T(8,128)S(1)}, u32[]{:S(2)}) copy-start(f32[1,784,384]{2,1,0:T(8,128)S(1)} %get-tuple-element.666) | copy-start | bytes 3612676
  327.5 38.6 %copy-start.89 = (f32[784]{0:T(1024)}, f32[784]{0:T(1024)S(1)}, u32[]{:S(2)}) copy-start(f32[784]{0:T(1024)S(1)} %broadcast_multiply_fusion.4) | copy-start | bytes 9412
  327.8 38.3 %copy-start.98 = (f32[784]{0:T(1024)}, f32[784]{0:T(1024)S(1)}, u32[]{:S(2)}) copy-start(f32[784]{0:T(1024)S(1)} %multiply_reduce_fusion.14) | copy-start | bytes 9412
  327.9 38.3 %copy-start.93 = (f32[784]{0:T(1024)}, f32[784]{0:T(1024)S(1)}, u32[]{:S(2)}) copy-start(f32[784]{0:T(1024)S(1)} %fusion.178) | copy-start | bytes 9412
  329.0 38.6 %copy-start.143 = (bf16[768,384]{1,0:T(8,128)(2,1)S(1)}, bf16[768,384]{1,0:T(8,128)(2,1)}, u32[]{:S(2)}) copy-start(bf16[768,384]{1,0:T(8,128)(2,1)} %param.55) | copy-start | bytes 1769476
  329.0 76.9 %reduce-scatter.13.cloned.1.call-start = ((), (), s32[]{:S(2)}) async-start(), calls=%async_computation.11 | async-start | bytes 3612672 | tf_op jit(solution)/shard_map/reduce_scatter | solution.py:199
  367.6 38.3 %copy-start.130 = (f32[384]{0:T(512)S(1)}, f32[384]{0:T(512)}, u32[]{:S(2)}) copy-start(f32[384]{0:T(512)} %param.56) | copy-start | bytes 4612
  370.5 37.3 %copy-start.105 = (f32[384]{0:T(512)S(1)}, f32[384]{0:T(512)}, u32[]{:S(2)}) copy-start(f32[384]{0:T(512)} %param.57) | copy-start | bytes 4612
  370.5 37.3 %copy-start.131 = (f32[384]{0:T(512)S(1)}, f32[384]{0:T(512)}, u32[]{:S(2)}) copy-start(f32[384]{0:T(512)} %param.58) | copy-start | bytes 4612
  370.5 38.5 %copy-start.136 = (f32[2,192]{1,0:T(2,128)S(1)}, f32[2,192]{1,0:T(2,128)}, u32[]{:S(2)}) copy-start(f32[2,192]{1,0:T(2,128)} %param.60) | copy-start | bytes 4612
  370.5 61.7 %copy-start.78 = (bf16[384,3,192]{0,2,1:T(8,128)(2,1)S(1)}, bf16[384,3,192]{0,2,1:T(8,128)(2,1)}, u32[]{:S(2)}) copy-start(bf16[384,3,192]{0,2,1:T(8,128)(2,1)} %param.59) | copy-start | bytes 1327108
  370.5 61.6 %all-gather.13.cloned.1.call-start = ((), (), s32[]{:S(2)}) async-start(), calls=%async_computation.12 | async-start | bytes 1806336 | tf_op jit(solution)/shard_map/all_gather | solution.py:140
  407.4 102.7 %copy-start.19 = (f32[1,784,384]{2,1,0:T(8,128)}, f32[1,784,384]{2,1,0:T(8,128)S(1)}, u32[]{:S(2)}) copy-start(f32[1,784,384]{2,1,0:T(8,128)S(1)} %get-tuple-element.662) | copy-start | bytes 3612676
  407.4 27.3 %copy-start.91 = (f32[784]{0:T(1024)}, f32[784]{0:T(1024)S(1)}, u32[]{:S(2)}) copy-start(f32[784]{0:T(1024)S(1)} %broadcast_multiply_fusion.3) | copy-start | bytes 9412
  407.8 26.9 %copy-start.100 = (f32[784]{0:T(1024)}, f32[784]{0:T(1024)S(1)}, u32[]{:S(2)}) copy-start(f32[784]{0:T(1024)S(1)} %multiply_reduce_fusion.13) | copy-start | bytes 9412
  407.8 26.9 %copy-start.95 = (f32[784]{0:T(1024)}, f32[784]{0:T(1024)S(1)}, u32[]{:S(2)}) copy-start(f32[784]{0:T(1024)S(1)} %fusion.179) | copy-start | bytes 9412
  408.9 101.2 %reduce-scatter.15.cloned.1.call-start = ((), (), s32[]{:S(2)}) async-start(), calls=%async_computation.13 | async-start | bytes 3612672 | tf_op jit(solution)/shard_map/reduce_scatter | solution.py:180
  468.8 41.3 %copy-start.132 = (f32[384]{0:T(512)S(1)}, f32[384]{0:T(512)}, u32[]{:S(2)}) copy-start(f32[384]{0:T(512)} %param.62) | copy-start | bytes 4612
  474.7 38.1 %copy-start.104 = (f32[384]{0:T(512)S(1)}, f32[384]{0:T(512)}, u32[]{:S(2)}) copy-start(f32[384]{0:T(512)} %param.63) | copy-start | bytes 4612
  474.7 38.1 %copy-start.133 = (f32[384]{0:T(512)S(1)}, f32[384]{0:T(512)}, u32[]{:S(2)}) copy-start(f32[384]{0:T(512)} %param.64) | copy-start | bytes 4612
  474.7 62.4 %copy-start.147 = (f32[768]{0:T(1024)S(1)}, f32[768]{0:T(1024)}, u32[]{:S(2)}) copy-start(f32[768]{0:T(1024)} %param.66) | copy-start | bytes 9220
  474.7 62.4 %all-gather.15.cloned.1.call-start = ((), (), s32[]{:S(2)}) async-start(), calls=%async_computation.14 | async-start | bytes 1806336 | tf_op jit(solution)/shard_map/all_gather | solution.py:140
  513.9 47.9 %all-gather.17.cloned.1.call-start = ((), (), s32[]{:S(2)}) async-start(), calls=%async_computation.16 | async-start | bytes 1806336 | tf_op jit(solution)/shard_map/all_gather | solution.py:251
  514.6 47.2 %copy-start.142 = (bf16[768,384]{1,0:T(8,128)(2,1)S(1)}, bf16[768,384]{1,0:T(8,128)(2,1)}, u32[]{:S(2)}) copy-start(bf16[768,384]{1,0:T(8,128)(2,1)} %param.67) | copy-start | bytes 1769476
  514.7 93.7 %reduce-scatter.19.cloned.1.call-start = ((), (), s32[]{:S(2)}) async-start(), calls=%async_computation.17 | async-start | bytes 3612672 | tf_op jit(solution)/shard_map/reduce_scatter | solution.py:144
  573.0 72.8 %reduce-scatter.17.cloned.1.call-start = ((), (), s32[]{:S(2)}) async-start(), calls=%async_computation.15 | async-start | bytes 3612672 | tf_op jit(solution)/shard_map/reduce_scatter | solution.py:199
  573.0 35.4 %copy-start.22 = (f32[1,784,384]{2,1,0:T(8,128)S(1)}, f32[1,784,384]{2,1,0:T(8,128)}, u32[]{:S(2)}) copy-start(f32[1,784,384]{2,1,0:T(8,128)} %copy-done.21) | copy-start | bytes 3612676
  577.7 68.0 %copy-start.134 = (f32[384]{0:T(512)S(1)}, f32[384]{0:T(512)}, u32[]{:S(2)}) copy-start(f32[384]{0:T(512)} %param.68) | copy-start | bytes 4612
  577.7 97.4 %all-gather.19.cloned.1.call-start = ((), (), s32[]{:S(2)}) async-start(), calls=%async_computation.18 | async-start | bytes 1806336 | tf_op jit(solution)/shard_map/all_gather | solution.py:271
  610.8 64.4 %copy-start.73 = (bf16[192,384]{1,0:T(8,128)(2,1)S(1)}, bf16[192,384]{1,0:T(8,128)(2,1)}, u32[]{:S(2)}) copy-start(bf16[192,384]{1,0:T(8,128)(2,1)} %param.61) | copy-start | bytes 442372
  648.7 31.5 %copy-start.102 = (f32[784]{0:T(1024)}, f32[784]{0:T(1024)S(1)}, u32[]{:S(2)}) copy-start(f32[784]{0:T(1024)S(1)} %negate_multiply_fusion.5) | copy-start | bytes 9412
  649.8 31.4 %copy-start.24 = (bf16[1568,192]{1,0:T(8,128)(2,1)S(1)}, bf16[1568,192]{1,0:T(8,128)(2,1)}, u32[]{:S(2)}) copy-start(bf16[1568,192]{1,0:T(8,128)(2,1)} %get-tuple-element.1225) | copy-start | bytes 1806340
  652.0 110.8 %reduce-scatter.21.cloned.1.call-start = ((), (), s32[]{:S(2)}) async-start(), calls=%async_computation.19 | async-start | bytes 3612672 | tf_op jit(solution)/shard_map/reduce_scatter | solution.py:144
  723.4 39.4 %copy-start.92 = (f32[784]{0:T(1024)S(1)}, f32[784]{0:T(1024)}, u32[]{:S(2)}) copy-start(f32[784]{0:T(1024)} %copy-done.91) | copy-start | bytes 9412
  723.4 39.4 %copy-start.96 = (f32[784]{0:T(1024)S(1)}, f32[784]{0:T(1024)}, u32[]{:S(2)}) copy-start(f32[784]{0:T(1024)} %copy-done.95) | copy-start | bytes 9412
  723.4 39.4 %copy-start.106 = (f32[384]{0:T(512)S(1)}, f32[384]{0:T(512)}, u32[]{:S(2)}) copy-start(f32[384]{0:T(512)} %param.57) | copy-start | bytes 4612
  727.4 35.4 %copy-start.20 = (f32[1,784,384]{2,1,0:T(8,128)S(1)}, f32[1,784,384]{2,1,0:T(8,128)}, u32[]{:S(2)}) copy-start(f32[1,784,384]{2,1,0:T(8,128)} %copy-done.19) | copy-start | bytes 3612676
  727.4 37.9 %copy-start.101 = (f32[784]{0:T(1024)S(1)}, f32[784]{0:T(1024)}, u32[]{:S(2)}) copy-start(f32[784]{0:T(1024)} %copy-done.100) | copy-start | bytes 9412
  727.4 38.5 %copy-start.32 = (f32[1,784,384]{2,1,0:T(8,128)S(1)}, f32[1,784,384]{2,1,0:T(8,128)}, u32[]{:S(2)}) copy-start(f32[1,784,384]{2,1,0:T(8,128)} %copy-done.31) | copy-start | bytes 3612676
  727.4 38.5 %copy-start.103 = (f32[784]{0:T(1024)S(1)}, f32[784]{0:T(1024)}, u32[]{:S(2)}) copy-start(f32[784]{0:T(1024)} %copy-done.102) | copy-start | bytes 9412
  727.4 65.8 %all-gather.21.cloned.1.call-start = ((), (), s32[]{:S(2)}) async-start(), calls=%async_computation.20 | async-start | bytes 1806336 | tf_op jit(solution)/shard_map/all_gather | solution.py:251
  765.9 27.3 %copy-start.144 = (bf16[768,384]{1,0:T(8,128)(2,1)S(1)}, bf16[768,384]{1,0:T(8,128)(2,1)}, u32[]{:S(2)}) copy-start(bf16[768,384]{1,0:T(8,128)(2,1)} %param.55) | copy-start | bytes 1769476
  765.9 27.3 %copy-start.149 = (f32[768]{0:T(1024)S(1)}, f32[768]{0:T(1024)}, u32[]{:S(2)}) copy-start(f32[768]{0:T(1024)} %param.54) | copy-start | bytes 9220
  770.0 69.8 %reduce-scatter.23.cloned.1.call-start = ((), (), s32[]{:S(2)}) async-start(), calls=%async_computation.21 | async-start | bytes 3612672 | tf_op jit(solution)/shard_map/reduce_scatter | solution.py:144
  801.5 38.3 %copy-start.90 = (f32[784]{0:T(1024)S(1)}, f32[784]{0:T(1024)}, u32[]{:S(2)}) copy-start(f32[784]{0:T(1024)} %copy-done.89) | copy-start | bytes 9412
  801.5 38.3 %copy-start.94 = (f32[784]{0:T(1024)S(1)}, f32[784]{0:T(1024)}, u32[]{:S(2)}) copy-start(f32[784]{0:T(1024)} %copy-done.93) | copy-start | bytes 9412
  801.5 38.3 %copy-start.108 = (f32[384]{0:T(512)S(1)}, f32[384]{0:T(512)}, u32[]{:S(2)}) copy-start(f32[384]{0:T(512)} %param.51) | copy-start | bytes 4612
  804.3 35.4 %copy-start.18 = (f32[1,784,384]{2,1,0:T(8,128)S(1)}, f32[1,784,384]{2,1,0:T(8,128)}, u32[]{:S(2)}) copy-start(f32[1,784,384]{2,1,0:T(8,128)} %copy-done.17) | copy-start | bytes 3612676
  804.3 37.9 %copy-start.99 = (f32[784]{0:T(1024)S(1)}, f32[784]{0:T(1024)}, u32[]{:S(2)}) copy-start(f32[784]{0:T(1024)} %copy-done.98) | copy-start | bytes 9412
  804.4 38.5 %copy-start.34 = (f32[1,784,384]{2,1,0:T(8,128)S(1)}, f32[1,784,384]{2,1,0:T(8,128)}, u32[]{:S(2)}) copy-start(f32[1,784,384]{2,1,0:T(8,128)} %copy-done.33) | copy-start | bytes 3612676
  804.4 64.5 %all-gather.23.cloned.1.call-start = ((), (), s32[]{:S(2)}) async-start(), calls=%async_computation.22 | async-start | bytes 1806336 | tf_op jit(solution)/shard_map/all_gather | solution.py:271
  842.9 26.0 %copy-start.75 = (bf16[192,384]{1,0:T(8,128)(2,1)S(1)}, bf16[192,384]{1,0:T(8,128)(2,1)}, u32[]{:S(2)}) copy-start(bf16[192,384]{1,0:T(8,128)(2,1)} %param.49) | copy-start | bytes 442372
  845.6 27.2 %copy-start.86 = (f32[2,2,784]{2,1,0:T(2,128)S(1)}, f32[2,2,784]{2,1,0:T(2,128)}, u32[]{:S(2)}) copy-start(f32[2,2,784]{2,1,0:T(2,128)} %copy-done.85) | copy-start | bytes 37636
  845.6 422.4 %reduce-scatter.25.cloned.1.call-start = ((), (), s32[]{:S(2)}) async-start(), calls=%async_computation.24 | async-start | bytes 9633792
  1155.4 210.1 %all-reduce.6.cloned.1.call-start = ((), (), s32[]{:S(2)}) async-start(), calls=%async_computation.23 | async-start | bytes 589824 | tf_op jit(solution)/shard_map/psum | solution.py:437
  1186.5 336.5 %all-reduce.8.cloned.1.call-start = ((), (), s32[]{:S(2)}) async-start(), calls=%async_computation.25 | async-start | bytes 13565952 | tf_op jit(solution)/shard_map/psum | solution.py:418
  1329.7 195.7 %copy-start.137 = (f32[384]{0:T(512)}, f32[384]{0:T(512)S(1)}, u32[]{:S(2)}) copy-start(f32[384]{0:T(512)S(1)} %get-tuple-element.1166) | copy-start | bytes 4612
  (131 other events, 691.8 us)
Sparse Core Ops, SparseCore 0:
  18.7 84.5 all-gather.8
  290.7 35.2 reduce-scatter.10
  329.1 23.0 all-gather.10
  370.6 35.2 reduce-scatter.12
  409.1 23.0 all-gather.12
  474.8 35.2 reduce-scatter.14
  514.0 23.0 all-gather.14
  538.7 23.0 all-gather.16
  573.1 35.2 reduce-scatter.18
  610.5 35.2 reduce-scatter.16
  652.1 23.0 all-gather.18
  727.5 35.2 reduce-scatter.20
  770.1 23.0 all-gather.20
  804.5 35.2 reduce-scatter.22
  845.8 23.0 all-gather.22
  1155.5 78.4 reduce-scatter.24
  1239.8 125.6 all-reduce.5
  1372.9 150.0 all-reduce.7
where the time goes:
time: 1550 us; the launch traced here: 1540 us
  waiting for transfers between devices  642 us (41%)
  matrix products  393 us (25%)
  local copies, waits for them, and re-layouts  198 us (13%)
  other arithmetic  189 us (12%)
  blocking collectives  98.7 us (6%)
  between operations  16.7 us (1%)
    psum x1, waiting for transfers between devices, shards(): lax.psum((split_first[0], split_first[1], split_first[2], split_first[3],...  158 us
    all_gather x4, waiting for transfers between devices, rows_gather(): return lax.all_gather(own_rows, 'head', axis=1, tiled=True)  150 us
    reduce_scatter x3, waiting for transfers between devices, rows_reduce(): lax.psum_scatter(partial_rows, 'head', scatter_dimension=1, tiled=True)  101 us
    convert_element_type x8, other arithmetic, one_block(): score_grads = (softmaxed * (prob_grads - row_inner)).astype(jnp.bfloat16)  72.3 us
    reduce_scatter x2, waiting for transfers between devices, layer_forward(): lax.psum_scatter(partial_feed, 'head', scatter_dimension=1, tiled=True)  70.2 us
    dot_general x8, matrix products, one_block(): jnp.einsum('qd,kd->qk', query_block[:, columns], key_rows[:, columns], pr...  68.3 us
    dot_general x8, matrix products, one_block(): jnp.einsum('qd,kd->qk', query_head, key_head, preferred_element_type=jnp....  63.5 us
    psum x1, blocking collectives, shards(): lax.psum((split_first[0], split_first[1], split_first[2], split_first[3],...  61.2 us
  transfers between devices with their start and end apart: 18, of which 17 were waited for; matrix products, arithmetic and copies ran while one was open for 8% of the time, Pallas kernels for 0%

commit v1 on v0

v1 whole, which is shorter than its diff:
```python
import functools

import jax
import jax.numpy as jnp
from jax import lax
from jax.experimental import pallas as pl
from jax.experimental.pallas import tpu as pltpu
from jax.sharding import Mesh, PartitionSpec as P

HEAD_DIM = 96
WIDE = 128
SIDE = 14
DEAD = -1e30
LOG2E = 1.4426950408889634
LN2 = 0.6931471805599453
SCALE = HEAD_DIM ** (-0.5)
EPS = 1e-06
CHUNK = 512
SAFE = 60.0
BATCH = ("outer", "core")

bf16 = jnp.bfloat16
f32 = jnp.float32


def dot(a, b):
    return jnp.dot(a, b, preferred_element_type=f32)


def dot_nt(a, b):
    return lax.dot_general(a, b, (((1,), (1,)), ((), ())), preferred_element_type=f32)


def flip(a):
    return a.astype(f32).T


def chunks(total):
    return [(start, min(CHUNK, total - start)) for start in range(0, total, CHUNK)]


def norm_stats(v):
    centered = v - jnp.mean(v, axis=-1, keepdims=True)
    rstd = lax.rsqrt(jnp.mean(centered * centered, axis=-1, keepdims=True) + EPS)
    return centered * rstd, rstd


def norm_back(xhat, rstd, gain, grad):
    scaled = grad * gain
    back = rstd * (
        scaled
        - jnp.mean(scaled, axis=-1, keepdims=True)
        - xhat * jnp.mean(scaled * xhat, axis=-1, keepdims=True)
    )
    return (
        back,
        jnp.sum(grad * xhat, axis=0, keepdims=True),
        jnp.sum(grad, axis=0, keepdims=True),
    )


def three_parts(v):
    high = v.astype(bf16).astype(f32)
    rest = v - high
    middle = rest.astype(bf16).astype(f32)
    return high, middle, rest - middle


def with_columns(block, first, column):
    lane = lax.broadcasted_iota(jnp.int32, block.shape, 1)
    for offset, part in enumerate(three_parts(column)):
        block = jnp.where(lane == first + offset, part, block)
    return block


def gelu_both(u):
    cdf = 0.5 + 0.5 * lax.erf(u * 0.7071067811865476)
    return u * cdf, cdf + u * (jnp.exp(-0.5 * u * u) * 0.3989422804014327)


NORM1, WIDEN_B, OUT_B1, MLP1, DOWN_B1, NORM2, OUT_B2, MLP2, DOWN_B2 = 0, 2, 3, 4, 6, 7, 9, 10, 12
SMEM = "smem"


def call(body, grid, ins, outs, scratch, micros, offset=0, megabytes=56):
    def spec(shape, block):
        if block == SMEM:
            return pl.BlockSpec(memory_space=pltpu.SMEM)
        if block is None:
            zeros = (0,) * len(shape)
            return pl.BlockSpec(tuple(shape), lambda *_: zeros)
        if block[0] == "own":
            rest = (0,) * (len(shape) - 1)
            return pl.BlockSpec(tuple(block[1:]), lambda i, *_: (i,) + rest)
        if block[0] == "half":
            rest = (0,) * (len(shape) - 1)
            return pl.BlockSpec(tuple(block[1:]), lambda i, *_: ((i + offset) // 2,) + rest)
        rest = (0,) * (len(shape) - 1)
        return pl.BlockSpec(tuple(block), lambda i, *_: (i + offset,) + rest)

    def out_spec(shape, block):
        if block is None or block[0] == "half":
            return spec(shape, block)
        rest = (0,) * (len(shape) - 1)
        return pl.BlockSpec(tuple(block), lambda i, *_: (i,) + rest)

    return pl.pallas_call(
        body,
        grid=grid,
        in_specs=[spec(a.shape, b) for a, b in ins],
        out_specs=[out_spec(s, b) for s, _, b in outs],
        out_shape=[jax.ShapeDtypeStruct(s, d) for s, d, _ in outs],
        scratch_shapes=scratch,
        cost_estimate=pl.CostEstimate(
            flops=int(micros * 1.15e9), transcendentals=0, bytes_accessed=int(micros * 3.69e6)
        ),
        compiler_params=pltpu.CompilerParams(
            dimension_semantics=("arbitrary",) * len(grid),
            vmem_limit_bytes=megabytes << 20,
        ),
    )(*[a for a, _ in ins])


def full(*arrays):
    return [(a, None) for a in arrays]


def dead_keys(spot, count, marks, keys, far):
    half = marks.shape[1] // 2
    each = keys // half
    first = (1 - spot[0] if far else spot[0]) * half
    lane = lax.broadcasted_iota(jnp.int32, (1, keys), 1)
    row = jnp.zeros((1, keys), f32)
    for f in range(half):
        dead = (first + f >= count[0]) | (marks[0, first + f] != 1)
        row = jnp.where((lane >= f * each) & (lane < (f + 1) * each), jnp.where(dead, DEAD, 0.0), row)
    return row


def head_forms(spot, w_own, w_far, pack_own, pack_far, layer, w_out, b_out):
    first = spot[1] == 0
    w_out[...] = jnp.zeros_like(w_out)
    b_out[...] = jnp.zeros_like(b_out)
    for side, (w, pack) in enumerate(((w_own, pack_own), (w_far, pack_far))):
        for j in range(3):
            low = w[j, :, :HEAD_DIM].astype(f32)
            high = w[j, :, HEAD_DIM:].astype(f32)
            lanes = slice(j * WIDE, j * WIDE + HEAD_DIM)
            w_out[2 * side, :, lanes] = jnp.where(first, low, high).astype(bf16)
            w_out[2 * side + 1, :, lanes] = jnp.where(first, high, low).astype(bf16)
        for j in range(2):
            start = (2 * layer + j) * 2 * HEAD_DIM
            low = pack[2:3, start : start + HEAD_DIM]
            high = pack[2:3, start + HEAD_DIM : start + 2 * HEAD_DIM]
            b_out[2 * side, j : j + 1, :HEAD_DIM] = jnp.where(first, low, high)
            b_out[2 * side + 1, j : j + 1, :HEAD_DIM] = jnp.where(first, high, low)


def project_keys(x_t, w, b, mask, kt_out, vt_out):
    both = dot(flip(w[:, WIDE:]).astype(bf16), x_t)
    k_t, v_t = both[:WIDE], both[WIDE:]
    key_bound = jnp.max(jnp.sum(k_t * k_t, axis=0, keepdims=True))
    row = lax.broadcasted_iota(jnp.int32, k_t.shape, 0)
    k_t = jnp.where(row == HEAD_DIM, mask, k_t)
    k_t = jnp.where((row > HEAD_DIM) & (row < HEAD_DIM + 4), 1.0, k_t)
    kt_out[0] = k_t.astype(bf16)
    column = jnp.broadcast_to(b[1:2], (WIDE, WIDE)).T[:, :1]
    row = lax.broadcasted_iota(jnp.int32, column.shape, 0)
    column = jnp.where((row >= HEAD_DIM) & (row < HEAD_DIM + 3), 1.0, column)
    vt_out[0] = (v_t + column).astype(bf16)
    return key_bound


def soft_part(q, key_bound, kt_ref, vt_ref, s_ref, o_ref, m_ref):
    total = kt_ref.shape[2]
    q_wide = q.astype(f32)
    bound = jnp.max(jnp.sum(q_wide * q_wide, axis=1, keepdims=True)) * key_bound
    safe = bound < SAFE * SAFE

    @pl.when(safe)
    def _():
        out = None
        for start, size in chunks(total):
            part = slice(start, start + size)
            p = jnp.exp2(dot(q, kt_ref[0, :, part])).astype(bf16)
            o = dot_nt(p, vt_ref[0, :, part])
            out = o if out is None else out + o
        o_ref[0] = out
        m_ref[0] = jnp.zeros_like(m_ref[0])

    @pl.when(jnp.logical_not(safe))
    def _():
        peak = None
        for start, size in chunks(total):
            s = dot(q, kt_ref[0, :, start : start + size])
            s_ref[:, start : start + size] = s
            top = jnp.max(s, axis=1, keepdims=True)
            peak = top if peak is None else jnp.maximum(peak, top)
        out = None
        for start, size in chunks(total):
            part = slice(start, start + size)
            p = jnp.exp2(s_ref[:, part] - peak).astype(bf16)
            o = dot_nt(p, vt_ref[0, :, part])
            out = o if out is None else out + o
        o_ref[0] = out
        m_ref[0] = peak


def queries(rows, w, b):
    q = (dot(rows, w[:, :WIDE]) + b[0:1]) * (SCALE * LOG2E)
    lane = lax.broadcasted_iota(jnp.int32, q.shape, 1)
    return jnp.where(lane == HEAD_DIM, 1.0, q).astype(bf16)


def fwd_own_first(
    spot, count, marks, clip, vec, target, w_own, w_far, pack_own, pack_far,
    x_out, xp_out, xpt_out, w_out, b_out, kt_out, vt_out, q_out, o_out, m_out,
    xt_s, s_s,
):
    head = pl.program_id(0)

    @pl.when(head == 0)
    def _():
        head_forms(spot, w_own, w_far, pack_own, pack_far, 0, w_out, b_out)
        width = clip.shape[1]
        xhat, _ = norm_stats(clip[...].astype(f32))
        x = xhat * vec[NORM1 : NORM1 + 1, :width] + vec[NORM1 + 1 : NORM1 + 2, :width]
        x = x.astype(bf16)
        x_out[...] = x
        xt_s[...] = flip(x).astype(bf16)
        picked = None
        for start, size in chunks(clip.shape[0]):
            lane = lax.broadcasted_iota(jnp.int32, (target.shape[0], size), 1) + start
            hot = jnp.where(lane == target[...], 1.0, 0.0).astype(bf16)
            part = dot(hot, x_out[start : start + size, :])
            picked = part if picked is None else picked + part
        xp_out[...] = picked.astype(bf16)
        xpt_out[...] = picked.T.astype(bf16)

    mask = dead_keys(spot, count, marks, clip.shape[0], False)
    w, b = w_out[head], b_out[head]
    bound = project_keys(xt_s[...], w, b, mask, kt_out, vt_out)
    q = queries(xp_out[...], w, b)
    q_out[0] = q
    soft_part(q, bound, kt_out, vt_out, s_s, o_out, m_out)


def fwd_own_second(
    spot, count, marks, x, w_own, w_far, pack_own, pack_far,
    w_out, b_out, kt_out, vt_out, q_out, o_out, m_out,
    xt_s, s_s,
):
    head = pl.program_id(0)

    @pl.when(head == 0)
    def _():
        head_forms(spot, w_own, w_far, pack_own, pack_far, 1, w_out, b_out)
        xt_s[...] = flip(x[...]).astype(bf16)

    mask = dead_keys(spot, count, marks, x.shape[0], False)
    w, b = w_out[head], b_out[head]
    bound = project_keys(xt_s[...], w, b, mask, kt_out, vt_out)
    q = queries(x[...], w, b)
    q_out[0] = q
    soft_part(q, bound, kt_out, vt_out, s_s, o_out, m_out)


def finish_head(q, o1, m1, o2, m2, att_out, attt_out, qb_out, qt_out):
    peak = jnp.maximum(m1, m2)
    o = o1 * jnp.exp2(m1 - peak) + o2 * jnp.exp2(m2 - peak)
    total = o[:, HEAD_DIM : HEAD_DIM + 1]
    att = (o / total).astype(bf16)
    att_out[0] = att
    attt_out[0] = flip(att).astype(bf16)
    lse = peak + jnp.log(total) * LOG2E
    q_wide = q.astype(f32)
    qb_out[0] = with_columns(q_wide, HEAD_DIM + 1, -lse).astype(bf16)
    qt_out[0] = q_wide.T.astype(bf16)


def fwd_far_first(
    spot, count, marks, clip, vec, w, b, q, o1, m1,
    x_out, kt_out, vt_out, att_out, attt_out, qb_out, qt_out,
    xt_s, s_s, o_s, m_s,
):
    @pl.when(pl.program_id(0) == 0)
    def _():
        width = clip.shape[1]
        xhat, _ = norm_stats(clip[...].astype(f32))
        x = xhat * vec[NORM1 : NORM1 + 1, :width] + vec[NORM1 + 1 : NORM1 + 2, :width]
        x = x.astype(bf16)
        x_out[...] = x
        xt_s[...] = flip(x).astype(bf16)

    mask = dead_keys(spot, count, marks, clip.shape[0], True)
    bound = project_keys(xt_s[...], w[0], b[0], mask, kt_out, vt_out)
    soft_part(q[0], bound, kt_out, vt_out, s_s, o_s, m_s)
    finish_head(q[0], o1[0], m1[0], o_s[0], m_s[0], att_out, attt_out, qb_out, qt_out)


def fwd_far_second(
    spot, count, marks, x, w, b, q, o1, m1,
    kt_out, vt_out, att_out, attt_out, qb_out, qt_out,
    xt_s, s_s, o_s, m_s,
):
    @pl.when(pl.program_id(0) == 0)
    def _():
        xt_s[...] = flip(x[...]).astype(bf16)

    mask = dead_keys(spot, count, marks, x.shape[0], True)
    bound = project_keys(xt_s[...], w[0], b[0], mask, kt_out, vt_out)
    soft_part(q[0], bound, kt_out, vt_out, s_s, o_s, m_s)
    finish_head(q[0], o1[0], m1[0], o_s[0], m_s[0], att_out, attt_out, qb_out, qt_out)


def attend_own(scalars, x, weights, packs, vec=None, target=None):
    heads = 4
    keys, width = x.shape
    rows = keys if target is None else target.shape[0]
    flat = (1, WIDE, keys)
    head_outs = [
        ((heads, width, 3 * WIDE), bf16, None),
        ((heads, 8, WIDE), f32, None),
        ((heads,) + flat[1:], bf16, flat),
        ((heads,) + flat[1:], bf16, flat),
        ((heads, rows, WIDE), bf16, (1, rows, WIDE)),
        ((heads, rows, WIDE), f32, (1, rows, WIDE)),
        ((heads, rows, 1), f32, (1, rows, 1)),
    ]
    scratch = [pltpu.VMEM((width, keys), bf16), pltpu.VMEM((rows, keys), f32)]
    micros = 5 + keys / 210
    if target is not None:
        ins = scalars + full(x, vec, target, *weights, *packs)
        outs = [
            ((keys, width), bf16, None),
            ((rows, width), bf16, None),
            ((width, rows), bf16, None),
        ] + head_outs
        return call(fwd_own_first, (heads,), ins, outs, scratch, micros)
    ins = scalars + full(x, *weights, *packs)
    return call(fwd_own_second, (heads,), ins, head_outs, scratch, micros)


def attend_far(scalars, x, w, b, q, o1, m1, vec=None):
    heads = w.shape[0]
    keys, width = x.shape
    rows = q.shape[1]
    flat = (1, WIDE, keys)
    head_ins = [
        (w, (1,) + w.shape[1:]),
        (b, (1,) + b.shape[1:]),
        (q, (1, rows, WIDE)),
        (o1, (1, rows, WIDE)),
        (m1, (1, rows, 1)),
    ]
    head_outs = [
        ((heads,) + flat[1:], bf16, flat),
        ((heads,) + flat[1:], bf16, flat),
        ((heads, rows, WIDE), bf16, (1, rows, WIDE)),
        ((heads, WIDE, rows), bf16, (1, WIDE, rows)),
        ((heads, rows, WIDE), bf16, (1, rows, WIDE)),
        ((heads, WIDE, rows), bf16, (1, WIDE, rows)),
    ]
    scratch = [
        pltpu.VMEM((width, keys), bf16),
        pltpu.VMEM((rows, keys), f32),
        pltpu.VMEM((1, rows, WIDE), f32),
        pltpu.VMEM((1, rows, 1), f32),
    ]
    micros = 6 + keys / 210
    if vec is not None:
        ins = scalars + full(x, vec) + head_ins
        outs = [((keys, width), bf16, None)] + head_outs
        return call(fwd_far_first, (heads,), ins, outs, scratch, micros)
    return call(fwd_far_second, (heads,), scalars + full(x) + head_ins, head_outs, scratch, micros)


def score_grads(qb, qt, do, dot_, kt, vt, dkv_s):
    q_all, qt_all, do_all, dot_all = qb[0], qt[0], do[0], dot_[0]
    dq = None
    for start, size in chunks(kt.shape[2]):
        part = slice(start, start + size)
        p = jnp.exp2(dot(q_all, kt[0, :, part]))
        ds = (p * dot(do_all, vt[0, :, part])).astype(bf16)
        dkv_s[WIDE:, part] = dot(dot_all, p.astype(bf16)).astype(bf16)
        dkv_s[:WIDE, part] = (dot(qt_all, ds) * LN2).astype(bf16)
        dq_part = dot_nt(ds, kt[0, :, part])
        dq = dq_part if dq is None else dq + dq_part
    return dq


def add_up(head, total, value):
    @pl.when(head == 0)
    def _():
        total[...] = value

    @pl.when(head > 0)
    def _():
        total[...] += value


def row_sums(columns):
    ones = jnp.ones((8, columns.shape[1]), bf16)
    return dot_nt(ones, columns)[0:1]


def bwd_far(first, last, qb, qt, do, dot_, kt, vt, w, x, *refs):
    if first:
        dxt_in = None
    else:
        dxt_in, refs = refs[0], refs[1:]
    dq_out, dw_out, dvs_out, dx_out, dxt_s, dkv_s = refs
    head = pl.program_id(0)
    dq_out[0] = score_grads(qb, qt, do, dot_, kt, vt, dkv_s)
    dxt = dot(w[0, :, WIDE:], dkv_s[...])
    dw_out[0, 0] = dot(dkv_s[:HEAD_DIM, :], x[...])
    dw_out[0, 1] = dot(dkv_s[WIDE : WIDE + HEAD_DIM, :], x[...])
    dvs_out[0] = jnp.broadcast_to(row_sums(dkv_s[WIDE:, :]), (8, WIDE))
    add_up(head, dxt_s, dxt if first else dxt + jnp.where(head == 0, 1.0, 0.0) * dxt_in[...])

    @pl.when(head == pl.num_programs(0) - 1)
    def _():
        if first and last:
            dx_out[...] = dxt_s[...].T.astype(bf16)
        else:
            dx_out[...] = dxt_s[...].astype(dx_out.dtype)


def near_head(
    spot, head, step, qb, qt, do, dot_, kt, vt, w, x, xq, dq_far, dw_far, dvs_far,
    gmy_out, goth_out, sums_out, dkv_s,
):
    dq = score_grads(qb, qt, do, dot_, kt, vt, dkv_s) + dq_far[0]
    dqt = (dq * SCALE).T.astype(bf16)
    grads = (
        dot(dqt[:HEAD_DIM, :], xq[...]),
        dot(dkv_s[:HEAD_DIM, :], x[...]) + dw_far[0, 0],
        dot(dkv_s[WIDE : WIDE + HEAD_DIM, :], x[...]) + dw_far[0, 1],
    )

    @pl.when(head % 2 == 0)
    def _():
        for j in range(3):
            gmy_out[0, j] = grads[j].astype(bf16)

    @pl.when(head % 2 == 1)
    def _():
        for j in range(3):
            goth_out[0, j] = grads[j].astype(bf16)

    @pl.when(step == 0)
    def _():
        sums_out[...] = jnp.zeros_like(sums_out)

    side = jnp.where(head < 2, spot[0], 1 - spot[0])
    piece = jnp.where(head % 2 == 0, spot[1], 1 - spot[1])
    quarter = 2 * side + piece
    put_row(sums_out, quarter, row_sums(dqt), WIDE)
    put_row(sums_out, 4 + quarter, row_sums(dkv_s[WIDE:, :]) + dvs_far[0, 0:1], WIDE)
    return dot(w[0, :, :WIDE], dqt), dot(w[0, :, WIDE:], dkv_s[...])


def bwd_own_second(
    spot, qb, qt, do, dot_, kt, vt, w, x, dq_far, dw_far, dvs_far,
    gmy_out, goth_out, sums_out, dx_out,
    dxt_s, dkv_s,
):
    head = pl.program_id(0)
    from_q, from_kv = near_head(
        spot, head, head, qb, qt, do, dot_, kt, vt, w, x, x, dq_far, dw_far, dvs_far,
        gmy_out, goth_out, sums_out, dkv_s,
    )
    add_up(head, dxt_s, from_q + from_kv)

    @pl.when(head == pl.num_programs(0) - 1)
    def _():
        dx_out[...] = dxt_s[...].T


def bwd_own_first(
    start, first, last, spot, qb, qt, do, dot_, kt, vt, w, x, xq, target, widen_grad,
    dq_far, dw_far, dvs_far, *refs,
):
    if not first:
        dxt_in, dxpt_in, sums_in, dxt_far, clip, vec = refs[:6]
        refs = refs[6:]
    gmy_out, goth_out, sums_out, refs = refs[0], refs[1], refs[2], refs[3:]
    if last:
        dx_out, dxt_s, dxpt_s, dkv_s = refs
    else:
        dxt_s, dxpt_s, dkv_s = refs
    step = pl.program_id(0)

    @pl.when(step == 0)
    def _():
        sums_out[...] = jnp.zeros_like(sums_out)
        if not first:
            sums_out[0:8] = sums_in[...]

    from_q, from_kv = near_head(
        spot, start + step, 1, qb, qt, do, dot_, kt, vt, w, x, xq, dq_far, dw_far, dvs_far,
        gmy_out, goth_out, sums_out, dkv_s,
    )

    @pl.when(step == 0)
    def _():
        dxt_s[...] = from_kv if first else from_kv + dxt_in[...]
        dxpt_s[...] = from_q + (widen_grad[...].T if first else dxpt_in[...])

    @pl.when(step > 0)
    def _():
        dxt_s[...] += from_kv
        dxpt_s[...] += from_q

    if not last:
        return

    @pl.when(step == pl.num_programs(0) - 1)
    def _():
        width = clip.shape[1]
        dxpt = dxpt_s[...].astype(bf16)
        for at, size in chunks(x.shape[0]):
            lane = lax.broadcasted_iota(jnp.int32, (target.shape[0], size), 1) + at
            hot = jnp.where(lane == target[...], 1.0, 0.0).astype(bf16)
            part = slice(at, at + size)
            grad = (dxt_s[:, part] + dxt_far[:, part].astype(f32) + dot(dxpt, hot)).T
            xhat, rstd = norm_stats(clip[part, :].astype(f32))
            dx_out[part, :], dgain, dbeta = norm_back(
                xhat, rstd, vec[NORM1 : NORM1 + 1, :width], grad
            )
            sums_out[8:9, :width] += dgain
            sums_out[9:10, :width] += dbeta


def back_ins(saved, parts, w, x):
    qb, qt, do, dot_ = saved
    kt, vt = parts
    rows, keys = qb.shape[1], x.shape[0]
    flat = (1, WIDE, keys)
    rtall, rflat = (1, rows, WIDE), (1, WIDE, rows)
    return [
        (qb, rtall), (qt, rflat), (do, rtall), (dot_, rflat),
        (kt, flat), (vt, flat), (w, (1,) + w.shape[1:]), (x, None),
    ]


def attend_back_far(saved, parts, w, x, start, count, before=None):
    heads = w.shape[0]
    last = start + count == heads
    rows = saved[0].shape[1]
    keys, width = x.shape
    ins = back_ins(saved, parts, w, x)
    if before is not None:
        ins += full(before)
    outs = [
        ((count, rows, WIDE), f32, (1, rows, WIDE)),
        ((count, 2, HEAD_DIM, width), f32, (1, 2, HEAD_DIM, width)),
        ((count, 8, WIDE), f32, (1, 8, WIDE)),
        ((keys, width), bf16, None)
        if count == heads
        else ((width, keys), bf16 if last else f32, None),
    ]
    scratch = [pltpu.VMEM((width, keys), f32), pltpu.VMEM((2 * WIDE, keys), bf16)]
    body = functools.partial(bwd_far, before is None, last)
    return call(body, (count,), ins, outs, scratch, 14 if count == heads else 1, start)


def attend_back_own(spot, saved, parts, w, x, far):
    dq_far, dw_far, dvs_far = far
    heads = w.shape[0]
    rows = saved[0].shape[1]
    keys, width = x.shape
    ins = [(spot, SMEM)] + back_ins(saved, parts, w, x)
    ins += [
        (dq_far, (1, rows, WIDE)),
        (dw_far, (1,) + dw_far.shape[1:]),
        (dvs_far, (1,) + dvs_far.shape[1:]),
    ]
    outs = [
        ((2, 3, HEAD_DIM, width), bf16, ("half", 1, 3, HEAD_DIM, width)),
        ((2, 3, HEAD_DIM, width), bf16, ("half", 1, 3, HEAD_DIM, width)),
        ((8, 3 * WIDE), f32, None),
        ((keys, width), f32, None),
    ]
    scratch = [pltpu.VMEM((width, keys), f32), pltpu.VMEM((2 * WIDE, keys), bf16)]
    return call(bwd_own_second, (heads,), ins, outs, scratch, 9 + keys / 105)


def attend_back_side(spot, saved, parts, w, x, far, pooled, start, before):
    dq_far, dw_far, dvs_far = far
    rows = saved[0].shape[1]
    keys, width = x.shape
    whole = lambda a: (a, ("own", 1) + a.shape[1:])
    ins = [(spot, SMEM)] + back_ins(saved, parts, w, x) + full(*pooled)
    ins += [whole(dq_far), whole(dw_far), whole(dvs_far)]
    first = before is None
    if not first:
        ins += full(*before)
    outs = [
        ((1, 3, HEAD_DIM, width), bf16, None),
        ((1, 3, HEAD_DIM, width), bf16, None),
        ((8 if first else 16, 3 * WIDE), f32, None),
    ]
    scratch = [pltpu.VMEM((2 * WIDE, keys), bf16)]
    totals = [(width, keys), (width, rows)]
    if first:
        outs += [(shape, f32, None) for shape in totals]
    else:
        outs.append(((keys, width), f32, None))
        scratch = [pltpu.VMEM(shape, f32) for shape in totals] + scratch
    body = functools.partial(bwd_own_first, start, first, not first)
    return call(body, (2,), ins, outs, scratch, 20 if first else 0.3, start)


def pieces(spot):
    order = (spot[1], 1 - spot[1])
    return [(2 * side + p, side, p, order[p]) for side in (0, 1) for p in (0, 1)]


def put_row(ref, row, value, width):
    at = lax.broadcasted_iota(jnp.int32, (ref.shape[0], width), 0)
    ref[:, :width] = jnp.where(at == row, value, ref[:, :width])


def get_row(ref, row):
    at = lax.broadcasted_iota(jnp.int32, ref.shape, 0)
    return jnp.sum(jnp.where(at == row, ref[...], 0.0), axis=0, keepdims=True)


def absolute(spot, side, index):
    return 2 * (spot[0] if side == 0 else 1 - spot[0]) + index


def lanes_of(index, size):
    return pl.ds(pl.multiple_of(index * size, size), size)


def pad_heads(spot, wo_own, wo_far, wo_s):
    wo_s[...] = jnp.zeros_like(wo_s)
    for place, side, _, index in pieces(spot):
        wo_s[place, :HEAD_DIM, :] = (wo_own, wo_far)[side][lanes_of(index, HEAD_DIM), :]


def out_branch(att, wo_s):
    total = None
    for head in range(att.shape[0]):
        part = dot(att[head], wo_s[head])
        total = part if total is None else total + part
    return total


def sort_far(spot, mine, other, far_s):
    far_s[spot[1]] = mine[...]
    far_s[1 - spot[1]] = other[...]


def mid_first(
    spot, att, wo_own, wo_far, xp, widen, vec, up_own, down_own, up_far, down_far, pack_own, pack_far,
    mid_out, yt_out, act_out, slope_out, layer_out, x2_out, wo_s,
):
    pad_heads(spot, wo_own, wo_far, wo_s)
    size = up_own.shape[1] // 2
    branch = out_branch(att, wo_s) + vec[OUT_B1 : OUT_B1 + 1]
    mid = (dot(xp[...], widen[...]) + vec[WIDEN_B : WIDEN_B + 1]) + branch
    mid_out[...] = mid
    xhat, _ = norm_stats(mid)
    y = (xhat * vec[MLP1 : MLP1 + 1] + vec[MLP1 + 1 : MLP1 + 2]).astype(bf16)
    yt_out[...] = flip(y).astype(bf16)
    feed = None
    for place, side, _, index in pieces(spot):
        lanes = lanes_of(index, size)
        up = (up_own, up_far)[side][:, lanes]
        down = (down_own, down_far)[side][:, lanes]
        hidden = dot(y, up) + (pack_own, pack_far)[side][0:1, lanes]
        act, slope = gelu_both(hidden)
        act = act.astype(bf16)
        act_out[:, place * size : (place + 1) * size] = act
        slope_out[:, place * size : (place + 1) * size] = slope.astype(bf16)
        part = dot_nt(act, down)
        feed = part if feed is None else feed + part
    layer = mid + feed + vec[DOWN_B1 : DOWN_B1 + 1]
    layer_out[...] = layer
    xhat, _ = norm_stats(layer)
    x2_out[...] = (xhat * vec[NORM2 : NORM2 + 1] + vec[NORM2 + 1 : NORM2 + 2]).astype(bf16)


def branch_back(gatt, att, attt, wo_s, do_out, dot_out, g_outs, at):
    for head in range(att.shape[0]):
        do = dot_nt(gatt, wo_s[head]).astype(bf16).astype(f32)
        inner = jnp.sum(do * att[head].astype(f32), axis=1, keepdims=True)
        do_out[head] = with_columns(do, HEAD_DIM, -inner).astype(bf16)
        dot_out[head] = do.T.astype(bf16)
        grad = dot(attt[head, :HEAD_DIM, :], gatt).astype(bf16)
        g_outs[head % 2][head // 2, at : at + HEAD_DIM, :] = grad


def mid_second(
    spot, att, attt, wo_own, wo_far, layer1, vec, up_own, down_own, mine, other,
    pack_own, pack_far, cot,
    y_out, dmid_out, do_out, dot_out, gmy_out, goth_out, small_out, wo_s, far_s,
):
    pad_heads(spot, wo_own, wo_far, wo_s)
    sort_far(spot, mine, other, far_s)
    size = up_own.shape[1] // 2
    width = cot.shape[1]
    g_outs = (gmy_out, goth_out)
    small_out[...] = jnp.zeros_like(small_out)
    mid = layer1[...] + (out_branch(att, wo_s) + vec[OUT_B2 : OUT_B2 + 1])
    xhat, rstd = norm_stats(mid)
    gain = vec[MLP2 : MLP2 + 1]
    y = (xhat * gain + vec[MLP2 + 1 : MLP2 + 2]).astype(bf16)
    yt = flip(y).astype(bf16)
    g_low = cot[...]
    g = g_low.astype(f32)
    gt = g.T.astype(bf16)
    feed = None
    dy = None
    for place, side, p, index in pieces(spot):
        lanes = lanes_of(index, size)
        up = (up_own, far_s.at[0])[side][:, lanes]
        down = (down_own, far_s.at[1])[side][:, lanes]
        hidden = dot(y, up) + (pack_own, pack_far)[side][1:2, lanes]
        act, slope = gelu_both(hidden)
        act = act.astype(bf16)
        dhid = (dot(g_low, down) * slope).astype(bf16)
        part = dot_nt(act, down)
        feed = part if feed is None else feed + part
        part = dot_nt(dhid, up)
        dy = part if dy is None else dy + part
        g_outs[p][side, :width, :] = dot(yt, dhid).astype(bf16)
        g_outs[p][side, width : 2 * width, :] = dot(gt, act).astype(bf16)
        row = 4 + absolute(spot, side, index)
        put_row(small_out, row, jnp.sum(dhid.astype(f32), axis=0, keepdims=True), size)
    y_out[...] = (mid + feed + vec[DOWN_B2 : DOWN_B2 + 1]).astype(bf16)
    back, dgain, dbeta = norm_back(xhat, rstd, gain, dy)
    dmid = g + back
    dmid_out[...] = dmid
    small_out[0:1] = jnp.sum(g, axis=0, keepdims=True)
    small_out[1:2] = dgain
    small_out[2:3] = dbeta
    small_out[3:4] = jnp.sum(dmid, axis=0, keepdims=True)
    branch_back(dmid.astype(bf16), att, attt, wo_s, do_out, dot_out, g_outs, 2 * width)


def mid_back(
    spot, dx_own, dx_far, layer1, vec, dmid2, act, slope, yt, mid,
    up_own, down_own, up_far, down_far, wo_own, wo_far, att, attt, xpt, widen,
    do_out, dot_out, gmy_out, goth_out, wgrad_out, small_out, wo_s, widen_s,
):
    pad_heads(spot, wo_own, wo_far, wo_s)
    size = up_own.shape[1] // 2
    width = layer1.shape[1]
    g_outs = (gmy_out, goth_out)
    small_out[...] = jnp.zeros_like(small_out)
    xhat, rstd = norm_stats(layer1[...])
    back, dgain2, dbeta2 = norm_back(
        xhat, rstd, vec[NORM2 : NORM2 + 1], dx_own[...] + dx_far[...].astype(f32)
    )
    g = dmid2[...] + back
    g_low = g.astype(bf16)
    gt = flip(g_low).astype(bf16)
    dy = None
    for place, side, p, index in pieces(spot):
        lanes = lanes_of(index, size)
        here = slice(place * size, (place + 1) * size)
        up = (up_own, up_far)[side][:, lanes]
        down = (down_own, down_far)[side][:, lanes]
        dhid = (dot(g_low, down) * slope[:, here].astype(f32)).astype(bf16)
        part = dot_nt(dhid, up)
        dy = part if dy is None else dy + part
        g_outs[p][side, :width, :] = dot(yt[...], dhid).astype(bf16)
        g_outs[p][side, width : 2 * width, :] = dot(gt, act[:, here]).astype(bf16)
        row = 4 + absolute(spot, side, index)
        put_row(small_out, row, jnp.sum(dhid.astype(f32), axis=0, keepdims=True), size)
    xhat, rstd = norm_stats(mid[...])
    back, dgain, dbeta = norm_back(xhat, rstd, vec[MLP1 : MLP1 + 1], dy)
    dmid = g + back
    small_out[0:1] = jnp.sum(g, axis=0, keepdims=True)
    small_out[1:2] = dgain
    small_out[2:3] = dbeta
    small_out[3:4] = jnp.sum(dmid, axis=0, keepdims=True)
    small_out[8:9] = dgain2
    small_out[9:10] = dbeta2
    gatt = dmid.astype(bf16)
    branch_back(gatt, att, attt, wo_s, do_out, dot_out, g_outs, 2 * width)
    widen_s[...] = dot(xpt[...], gatt)
    rows = widen_s.shape[0] // 4
    at = 2 * width + HEAD_DIM
    for place, side, p, index in pieces(spot):
        quarter = widen_s[lanes_of(absolute(spot, side, index), rows), :]
        g_outs[p][side, at : at + rows, :] = quarter.astype(bf16)
    wgrad_out[...] = dot_nt(gatt, widen[...])


def finish_mlp(spot, mine, other, *refs):
    if len(refs) == 3:
        widen_far, widen_out = None, None
        up_out, down_out, out_out = refs
    else:
        widen_far, up_out, down_out, out_out, widen_out = refs
    width = up_out.shape[0]
    size = up_out.shape[1] // 2
    for part, index in ((mine, spot[1]), (other, 1 - spot[1])):
        lanes = lanes_of(index, size)
        up_out[:, lanes] = part[:width, :].astype(f32)
        down_out[lanes, :] = part[width : 2 * width, :].astype(f32).T
        out_out[lanes_of(index, HEAD_DIM), :] = part[2 * width : 2 * width + HEAD_DIM, :].astype(f32)
    if widen_out is not None:
        rows = widen_out.shape[0] // 4
        at = 2 * width + HEAD_DIM
        for side in (0, 1):
            for p, index in ((0, spot[1]), (1, 1 - spot[1])):
                if side == 0:
                    value = (mine, other)[p][at : at + rows, :]
                else:
                    value = widen_far[p]
                widen_out[lanes_of(absolute(spot, side, index), rows), :] = value.astype(f32)


def finish_qkv(spot, mine, other, out, both_s):
    for j in range(3):
        for part, index in ((mine, spot[1]), (other, 1 - spot[1])):
            both_s[lanes_of(index, HEAD_DIM), :] = part[j].astype(f32)
        out[:, j, :] = both_s[...].T


def finish_small(spot, small, *outs):
    (n1g, n1b, wb, qvb1, ob1, m1g, m1b, ub1, db1, n2g, n2b, qvb2, ob2, m2g, m2b, ub2, db2) = outs
    first = 2 * spot[0]

    def put(out, row):
        out[...] = small[row, : out.shape[0]]

    def put_layer(base, sums, ub, qvb):
        size = ub.shape[0] // 2
        for p in (0, 1):
            ub[p * size : (p + 1) * size] = get_row(small, base + 4 + first + p)[0]
            for j in (0, 1):
                row = get_row(small, sums + 4 * j + first + p)
                qvb[j : j + 1, p * HEAD_DIM : (p + 1) * HEAD_DIM] = row[:, :HEAD_DIM]

    put(db2, 0)
    put(m2g, 1)
    put(m2b, 2)
    put(ob2, 3)
    put(db1, 16)
    put(m1g, 17)
    put(m1b, 18)
    put(ob1, 19)
    put(wb, 19)
    put(n2g, 24)
    put(n2b, 25)
    put(n1g, 48)
    put(n1b, 49)
    put_layer(0, 32, ub2, qvb2)
    put_layer(16, 40, ub1, qvb1)


def swap(x):
    return lax.ppermute(x, "head", [(0, 1), (1, 0)])


def core_swap(x):
    return lax.ppermute(x, "core", [(0, 1), (1, 0)])


def add_low(a, b):
    return (a.astype(f32) + b.astype(f32)).astype(bf16)


def tie(later, dep):
    return lax.optimization_barrier((later, dep))


def exchange(x, axis, bit):
    other = lax.ppermute(x, axis, [(i, i ^ bit) for i in range(lax.axis_size(axis))])
    return (x.astype(f32) + other.astype(f32)).astype(x.dtype)


def exchange_bits(axis):
    bits = [1 << k for k in range((lax.axis_size(axis) - 1).bit_length())]
    return bits[1:] + bits[:1]


def tree_sum(x, axis):
    for bit in exchange_bits(axis):
        x = exchange(x, axis, bit)
    return x


def shards(
    clip_in,
    frame_count,
    frame_mask,
    pool_index,
    first_norm_gain,
    first_norm_bias,
    first_widen_weight,
    first_widen_bias,
    first_qkv_weight,
    first_qv_bias,
    first_out_weight,
    first_out_bias,
    first_mlp_gain,
    first_mlp_bias,
    first_up_weight,
    first_up_bias,
    first_down_weight,
    first_down_bias,
    second_norm_gain,
    second_norm_bias,
    second_qkv_weight,
    second_qv_bias,
    second_out_weight,
    second_out_bias,
    second_mlp_gain,
    second_mlp_bias,
    second_up_weight,
    second_up_bias,
    second_down_weight,
    second_down_bias,
    cotangent,
):
    clip = clip_in[0]
    cot = cotangent[0]
    side = lax.axis_index("head")
    spot = jnp.stack([side, lax.axis_index("core")]).astype(jnp.int32)
    scalars = [(spot, SMEM), (frame_count, SMEM), (frame_mask, SMEM)]
    place = (spot, SMEM)
    keys1, width1 = clip.shape
    rows, dim = cot.shape
    n_up = first_up_bias.shape[0]
    hidden = 2 * n_up
    heads = 4
    out_rows = 2 * dim + HEAD_DIM
    half_up = n_up // 2

    qkv1 = jnp.swapaxes(first_qkv_weight, 0, 1)
    qkv2 = jnp.swapaxes(second_qkv_weight, 0, 1)
    qv_row = jnp.concatenate([first_qv_bias.reshape(-1), second_qv_bias.reshape(-1)])
    pack = jnp.stack([first_up_bias, second_up_bias, qv_row])
    far_qkv1 = swap(qkv1)
    far_pack = swap(pack)
    clip_send, (far_qkv1, far_pack) = tie(clip, (far_qkv1, far_pack))
    far_clip = swap(clip_send)
    down1, down2 = first_down_weight.T, second_down_weight.T
    first_core = lax.axis_index("core") == 0
    send2 = jnp.where(first_core, second_up_weight, down2)

    def wide(v):
        return jnp.pad(v, (0, dim - v.shape[0]))

    vec = jnp.stack(
        [
            wide(first_norm_gain), wide(first_norm_bias), first_widen_bias, first_out_bias,
            first_mlp_gain, first_mlp_bias, first_down_bias, second_norm_gain, second_norm_bias,
            second_out_bias, second_mlp_gain, second_mlp_bias, second_down_bias,
        ]
    )

    picks = lax.dynamic_slice_in_dim(pool_index[0], side * rows, rows, 0)
    token = jnp.arange(rows, dtype=jnp.int32)
    frame, cell = token // (SIDE * SIDE), token % (SIDE * SIDE)
    line = 2 * (cell // SIDE) + picks // 2
    column = 2 * (cell % SIDE) + picks % 2
    target = (frame * (4 * SIDE * SIDE) + line * (2 * SIDE) + column)[:, None]

    x1, x1p, x1pt, w1, b1, kt1, vt1, q1, o1, m1 = attend_own(
        scalars, clip, (qkv1, far_qkv1), (pack, far_pack), vec, target
    )
    mlp1, m1 = tie((first_out_weight, first_up_weight, down1), m1)
    far_out1, far_up1, far_down1 = [swap(w) for w in mlp1]
    x1f, kt1f, vt1f, att1, attt1, qb1, qt1 = attend_far(
        scalars, far_clip, w1, b1, q1, o1, m1, vec
    )
    late, att1 = tie((qkv2, second_out_weight), att1)
    far_qkv2, far_out2 = [swap(w) for w in late]
    send2, far_qkv2 = tie(send2, far_qkv2)
    mine2 = swap(send2)
    mid1, yt1, act1, slope1, layer1, x2 = call(
        mid_first,
        (),
        [place]
        + full(
            att1, first_out_weight, far_out1, x1p, first_widen_weight, vec,
            first_up_weight, down1, far_up1, far_down1, pack, far_pack,
        ),
        [
            ((rows, dim), f32, None),
            ((dim, rows), bf16, None),
            ((rows, hidden), bf16, None),
            ((rows, hidden), bf16, None),
            ((rows, dim), f32, None),
            ((rows, dim), bf16, None),
        ],
        [pltpu.VMEM((heads, WIDE, dim), bf16)],
        11,
    )

    x2f = swap(x2)
    w2, b2, kt2, vt2, q2, o2, m2 = attend_own(scalars, x2, (qkv2, far_qkv2), (pack, far_pack))
    far_out2, m2 = tie(far_out2, m2)
    kt2f, vt2f, att2, attt2, qb2, qt2 = attend_far(scalars, x2f, w2, b2, q2, o2, m2)
    mine2, att2 = tie(mine2, att2)
    other2 = core_swap(mine2)
    out, dmid2, do2, dot2, gmy2, goth2, small2 = call(
        mid_second,
        (),
        [place]
        + full(
            att2, attt2, second_out_weight, far_out2, layer1, vec, second_up_weight, down2,
            mine2, other2, pack, far_pack, cot,
        ),
        [
            ((rows, dim), bf16, None),
            ((rows, dim), f32, None),
            ((heads, rows, WIDE), bf16, None),
            ((heads, WIDE, rows), bf16, None),
            ((2, out_rows, half_up), bf16, None),
            ((2, out_rows, half_up), bf16, None),
            ((16, dim), f32, None),
        ],
        [pltpu.VMEM((heads, WIDE, dim), bf16), pltpu.VMEM((2, dim, n_up), bf16)],
        18,
    )

    got_a = core_swap(goth2)
    saved2 = (qb2, qt2, do2, dot2)
    dq2f, dw2f, dvs2f, dx2_send = attend_back_far(saved2, (kt2f, vt2f), w2, x2f, 0, heads)
    dx2_far = swap(dx2_send)
    near_a, away_a = add_low(gmy2[0], got_a[0]), add_low(gmy2[1], got_a[1])
    (near_a, away_a), dq2f = tie((near_a, away_a), dq2f)
    hmy2, hoth2, sums2, dx2 = attend_back_own(
        spot, saved2, (kt2, vt2), w2, x2, (dq2f, dw2f, dvs2f)
    )
    (away_a, hoth2), dx2 = tie((away_a, hoth2), dx2)
    got_a2 = swap(away_a)
    got_h2 = core_swap(hoth2)

    widen_rows = width1 // 4
    do1, dot1, gmy1, goth1, wgrad, small1 = call(
        mid_back,
        (),
        [place]
        + full(
            dx2, dx2_far, layer1, vec, dmid2, act1, slope1, yt1, mid1,
            first_up_weight, down1, far_up1, far_down1,
            first_out_weight, far_out1, att1, attt1, x1pt, first_widen_weight,
        ),
        [
            ((heads, rows, WIDE), bf16, None),
            ((heads, WIDE, rows), bf16, None),
            ((2, out_rows + widen_rows, half_up), bf16, None),
            ((2, out_rows + widen_rows, half_up), bf16, None),
            ((rows, width1), f32, None),
            ((16, dim), f32, None),
        ],
        [
            pltpu.VMEM((heads, WIDE, dim), bf16),
            pltpu.VMEM((width1, dim), f32),
        ],
        17,
    )
    near_h, away_h = add_low(hmy2[0], got_h2[0]), add_low(hmy2[1], got_h2[1])
    total_a = add_low(near_a, got_a2)
    (total_a, near_h, away_h, goth1), do1 = tie((total_a, near_h, away_h, goth1), do1)
    bits = exchange_bits("outer")
    next_a = exchange(total_a, "outer", bits[0])
    got_b = core_swap(goth1)
    got_h = swap(away_h)

    saved1 = (qb1, qt1, do1, dot1)
    two = heads // 2
    *own_far, dx1_part = attend_back_far(saved1, (kt1f, vt1f), w1, x1f, 0, two)
    near_b, away_b = add_low(gmy1[0], got_b[0]), add_low(gmy1[1], got_b[1])
    total_h = add_low(near_h, got_h)
    (near_b, away_b, total_h, next_a), dx1_part = tie((near_b, away_b, total_h, next_a), dx1_part)
    got_b2 = swap(away_b)
    next_a = exchange(next_a, "outer", bits[1])
    *far_far, dx1_send = attend_back_far(saved1, (kt1f, vt1f), w1, x1f, two, two, dx1_part)
    dx1_far = swap(dx1_send)
    total_b = add_low(near_b, got_b2)
    (next_a, total_b, total_h), far_far = tie((next_a, total_b, total_h), far_far)
    total_b, total_h = lax.psum((total_b, total_h), "outer")
    for bit in bits[2:]:
        next_a = exchange(next_a, "outer", bit)
    pooled = (x1p, target, wgrad)
    gmy_f, goth_f, sums1f, *totals = attend_back_side(
        spot, saved1, (kt1, vt1), w1, x1, far_far, pooled, two, None
    )
    (dx1_far, goth_f, total_a), own_far = tie((dx1_far, goth_f, next_a), own_far)
    other_a = core_swap(total_a)
    got_cf = core_swap(goth_f)
    gmy_o, goth_o, sums1, grad_in = attend_back_side(
        spot, saved1, (kt1, vt1), w1, x1, own_far, pooled, 0, (*totals, sums1f, dx1_far, clip, vec)
    )

    got_co = core_swap(goth_o)
    got_c2 = swap(add_low(gmy_f[0], got_cf[0]))
    total_c = (gmy_o[0].astype(f32) + got_co[0].astype(f32)).astype(bf16)
    total_c = add_low(total_c, got_c2)
    (total_b, total_h), total_c = tie((total_b, total_h), total_c)
    total_c = tree_sum(total_c, "outer")
    small = jnp.concatenate([small2, small1, sums2, sums1])
    small = tree_sum(small, "core")
    small = tree_sum(small, "head")
    small = tree_sum(small, "outer")

    def qkv_form(mine):
        width = mine.shape[2]
        (grad,) = call(
            finish_qkv,
            (),
            [place] + full(mine, core_swap(mine)),
            [((width, 3, 2 * HEAD_DIM), f32, None)],
            [pltpu.VMEM((2 * HEAD_DIM, width), f32)],
            2,
        )
        return grad

    mlp_outs = [
        ((dim, n_up), f32, None),
        ((n_up, dim), f32, None),
        ((2 * HEAD_DIM, dim), f32, None),
    ]
    gup2, gdn2, gout2 = call(
        finish_mlp, (), [place] + full(total_a, other_a), mlp_outs, [], 3
    )
    other_b = core_swap(total_b)
    widen_far = swap(jnp.stack([total_b[out_rows:], other_b[out_rows:]]))
    gup1, gdn1, gout1, gwiden = call(
        finish_mlp,
        (),
        [place] + full(total_b, other_b, widen_far),
        mlp_outs + [((width1, dim), f32, None)],
        [],
        3,
    )
    gqkv2 = qkv_form(total_h)
    gqkv1 = qkv_form(total_c)
    vector = ((dim,), f32, None)
    thin = ((width1,), f32, None)
    layer_vectors = [((2, 2 * HEAD_DIM), f32, None)] + [vector] * 3 + [((n_up,), f32, None), vector]
    (n1g, n1b, wb, qvb1, ob1, m1g, m1b, ub1, db1, n2g, n2b, qvb2, ob2, m2g, m2b, ub2, db2) = call(
        finish_small,
        (),
        [place] + full(small),
        [thin, thin, vector] + layer_vectors + [vector, vector] + layer_vectors,
        [],
        2,
    )
    return (
        out[None], grad_in[None],
        n1g, n1b, gwiden, wb, gqkv1, qvb1, gout1, ob1, m1g, m1b, gup1, ub1, gdn1, db1,
        n2g, n2b, gqkv2, qvb2, gout2, ob2, m2g, m2b, gup2, ub2, gdn2, db2,
    )


def solution(mesh):
    in_specs = (
        P(BATCH, "head", None),
        P(BATCH),
        P(BATCH, None),
        P(BATCH, None),
        P(),
        P(),
        P(),
        P(),
        P(None, None, "head"),
        P(None, "head"),
        P("head", None),
        P(),
        P(),
        P(),
        P(None, "head"),
        P("head"),
        P("head", None),
        P(),
        P(),
        P(),
        P(None, None, "head"),
        P(None, "head"),
        P("head", None),
        P(),
        P(),
        P(),
        P(None, "head"),
        P("head"),
        P("head", None),
        P(),
        P(BATCH, "head", None),
    )
    out_specs = (
        P(BATCH, "head", None),
        P(BATCH, "head", None),
        P(),
        P(),
        P(),
        P(),
        P(None, None, "head"),
        P(None, "head"),
        P("head", None),
        P(),
        P(),
        P(),
        P(None, "head"),
        P("head"),
        P("head", None),
        P(),
        P(),
        P(),
        P(None, None, "head"),
        P(None, "head"),
        P("head", None),
        P(),
        P(),
        P(),
        P(None, "head"),
        P("head"),
        P("head", None),
        P(),
    )
    outer = mesh.shape["batch"] // 2
    split = Mesh(
        mesh.devices.reshape(outer, 2, mesh.shape["head"]), ("outer", "core", "head")
    )
    return jax.shard_map(shards, mesh=split, in_specs=in_specs, out_specs=out_specs, check_vma=False)
```

time: 1550 us -> 392 us (0.25)
  waiting for transfers between devices: 642 us -> 34.5 us
  matrix products: 393 us -> 0 us
  Pallas kernels: 0 us -> 269 us
  other arithmetic: 189 us -> 7.48 us
  local copies, waits for them, and re-layouts: 198 us -> 30.9 us
  blocking collectives: 98.7 us -> 0 us
  starting transfers between devices: 1.38 us -> 34.5 us
    dot_general x80 -> x0, matrix products: 387 us -> none  [the longest x8 68.3 us: one_block(): jnp.einsum('qd,kd->qk', query_block[:, columns], key_rows[:, columns], pr...]
    pallas_call x0 -> x18, Pallas kernels: none -> 269 us  [call(): pl.pallas_call(body, grid=grid, in_specs=[spec(a.shape, b) for a, b in in...]
    all_gather x8 -> x0, waiting for transfers between devices: 229 us -> none  [the longest x4 150 us: rows_gather(): return lax.all_gather(own_rows, 'head', axis=1, tiled=True)]
    reduce_scatter x7 -> x0, waiting for transfers between devices: 223 us -> none  [the longest x3 101 us: rows_reduce(): lax.psum_scatter(partial_rows, 'head', scatter_dimension=1, tiled=True)]
    psum x2 -> x1, waiting for transfers between devices: 189 us -> 15.9 us  [shards(): total_b, total_h = lax.psum((total_b, total_h), 'outer')]
    psum x2 -> x0, blocking collectives: 98.7 us -> none  [the longest x1 61.2 us: shards(): lax.psum((split_first[0], split_first[1], split_first[2], split_first[3],...]
    convert_element_type x20 -> x14, other arithmetic: 91.6 us -> 3.5 us  [the longest x8 2.87 us: add_low(): return (a.astype(f32) + b.astype(f32)).astype(bf16)]
    reduce_sum x27 -> x0, other arithmetic: 72.3 us -> none  [the longest x4 24.3 us: one_block(): row_total = jnp.sum(weights, axis=1, keepdims=True)]
  transfers between devices with their start and end apart: 18 -> 39, of which waited for: 17 -> 9; matrix products, arithmetic and copies ran while one was open for 8% -> 6% of each run, Pallas kernels for 0% -> 63%
where the time goes in v1:
time: 392 us
  Pallas kernels  269 us (69%)
  starting transfers between devices  34.5 us (9%)
  waiting for transfers between devices  34.5 us (9%)
  local copies, waits for them, and re-layouts  30.9 us (8%)
  between operations  15.9 us (4%)
  other arithmetic  7.48 us (2%)
    pallas_call x18, Pallas kernels, call(): pl.pallas_call(body, grid=grid, in_specs=[spec(a.shape, b) for a, b in in...  269 us
    unnamed x112, local copies, waits for them, and re-layouts  19.8 us
    ppermute x17, starting transfers between devices, swap(): return lax.ppermute(x, 'head', [(0, 1), (1, 0)])  19.3 us
    ppermute x11, waiting for transfers between devices, exchange(): lax.ppermute(x, axis, [(i, i ^ bit) for i in range(lax.axis_size(axis))])  16.4 us
    psum x1, waiting for transfers between devices, shards(): total_b, total_h = lax.psum((total_b, total_h), 'outer')  15.9 us
    ppermute x11, starting transfers between devices, exchange(): lax.ppermute(x, axis, [(i, i ^ bit) for i in range(lax.axis_size(axis))])  13.6 us
  transfers between devices with their start and end apart: 39, of which 9 were waited for; matrix products, arithmetic and copies ran while one was open for 6% of the time, Pallas kernels for 63%

profile of v1, /device:TPU:0, one launch (start us, length us, event | category | flops | bytes accessed | tf_op | source)
XLA Modules:
  0.0 391.7 jit_solution(3403812178097277190)
XLA Ops:
  7.3 0.8 reshape.298
  8.1 0.8 reshape.299
  10.3 3.0 collective-permute-start.1
  13.7 1.8 fusion.12.target
  15.9 0.9 broadcast_select_fusion
  18.4 1.1 copy.85
  19.7 1.3 copy.79
  21.1 1.3 stack.92.vec.refs_5_
  22.4 1.9 copy.80
  24.3 1.9 collective-permute-start.2
  26.3 29.3 %shard_map.510 = (bf16[3136,192]{1,0:T(8,128)(2,1)}, bf16[784,192]{1,0:T(8,128)(2,1)}, bf16[192,784]{1,0:T(8,128)(2,1)}, bf16[4,192,384]{2,1,0:T(8,128)(2,1)}, f...) custom-call(s32[2]{0:T(128)} %pad_add_fusion.spot, ...), custom_call_target="tpu_custom_call" | custom-call | flops 22923333632 | bytes 73554000 | tf_op jit(solution)/shard_map/pallas_call | solution.py:107
  55.8 1.9 collective-permute-start.6
  57.8 1.7 copy.86.clip
  59.5 29.1 %shard_map.511 = (bf16[3136,192]{1,0:T(8,128)(2,1)}, bf16[4,128,3136]{2,1,0:T(8,128)(2,1)}, bf16[4,128,3136]{2,1,0:T(8,128)(2,1)}, bf16[4,784,128]{2,1,0:T(8,128...) custom-call(s32[2]{0:T(128)} %pad_add_fusion.spot, ...), custom_call_target="tpu_custom_call" | custom-call | flops 24073332736 | bytes 77244000 | tf_op jit(solution)/shard_map/pallas_call | solution.py:107
  88.6 2.0 collective-permute-start.9
  91.1 0.8 copy-done.41
  91.9 11.0 %shard_map.512 = (f32[784,384]{1,0:T(8,128)}, bf16[384,784]{1,0:T(8,128)(2,1)}, bf16[784,1536]{1,0:T(8,128)(2,1)}, bf16[784,1536]{1,0:T(8,128)(2,1)}, f32[784,384]{1,0:T(8,128)}, /*index=5*/bf16[784,384]{1,0:T(8,128)(2,1)}) custom-call(s32[2]{0:T(128)} %pad_add_fusion.spot, bf16[4,784,128]{2,1,0:T(8,128)(2,1)} %get-tuple-element.185.att, ...), custom_call_target="tpu_custom_call" | custom-call | flops 12650000384 | bytes 40590000 | tf_op jit(solution)/shard_map/pallas_call | solution.py:107
  102.9 1.9 collective-permute-start.8
  104.8 1.1 copy.88.w_far
  106.0 13.5 %shard_map.513 = (bf16[4,384,384]{2,1,0:T(8,128)(2,1)}, f32[4,8,128]{2,1,0:T(8,128)}, bf16[4,128,784]{2,1,0:T(8,128)(2,1)}, bf16[4,128,784]{2,1,0:T(8,128)(2,1)}...) custom-call(s32[2]{0:T(128)} %pad_add_fusion.spot, s32[1]{0:T(128)S(6)} %copy.97.count, ...), custom_call_target="tpu_custom_call" | custom-call | flops 10043333632 | bytes 32226000 | tf_op jit(solution)/shard_map/pallas_call | solution.py:107
  119.6 0.8 copy-done.39
  120.4 14.1 %shard_map.514 = (bf16[4,128,784]{2,1,0:T(8,128)(2,1)}, bf16[4,128,784]{2,1,0:T(8,128)(2,1)}, bf16[4,784,128]{2,1,0:T(8,128)(2,1)}, bf16[4,128,784]{2,1,0:T(8,12...) custom-call(s32[2]{0:T(128)} %pad_add_fusion.spot, s32[1]{0:T(128)S(6)} %copy.97.count, ...), custom_call_target="tpu_custom_call" | custom-call | flops 11193333760 | bytes 35916000 | tf_op jit(solution)/shard_map/pallas_call | solution.py:107
  134.7 2.0 collective-permute-done.10.other
  136.7 0.8 copy-done.43
  137.5 18.8 %shard_map.515 = (bf16[784,384]{1,0:T(8,128)(2,1)}, f32[784,384]{1,0:T(8,128)}, bf16[4,784,128]{2,1,0:T(8,128)(2,1)}, bf16[4,128,784]{2,1,0:T(8,128)(2,1)}, bf16...) custom-call(s32[2]{0:T(128)} %pad_add_fusion.spot, ...), custom_call_target="tpu_custom_call" | custom-call | flops 20700000256 | bytes 66420000 | tf_op jit(solution)/shard_map/pallas_call | solution.py:107
  156.4 13.7 %shard_map.516 = (f32[4,784,128]{2,1,0:T(8,128)}, f32[4,2,96,384]{3,2,1,0:T(8,128)}, f32[4,8,128]{2,1,0:T(8,128)}, bf16[784,384]{1,0:T(8,128)(2,1)}) custom-call(bf16[4,784,128]{2,1,0:T(8,128)(2,1)} %get-tuple-element.210.qb, bf16[4,128,784]{2,1,0:T(8,128)(2,1)} %get-tuple-element.211.qt, bf16[4,784,128]{2,1,0:T(8,128)(2,1)} %get-tuple-element.212.do, ...), custom_call_target="tpu_custom_call" | custom-call | flops 16099999744 | bytes 51660000 | tf_op jit(solution)/shard_map/pallas_call | solution.py:107
  170.1 2.0 collective-permute-start.14
  172.5 17.8 %shard_map.517 = (bf16[2,3,96,384]{3,2,1,0:T(8,128)(2,1)}, bf16[2,3,96,384]{3,2,1,0:T(8,128)(2,1)}, f32[8,384]{1,0:T(8,128)}, f32[784,384]{1,0:T(8,128)}) custom-call(s32[2]{0:T(128)} %pad_add_fusion.spot, bf16[4,784,128]{2,1,0:T(8,128)(2,1)} %get-tuple-element.210.qb, bf16[4,128,784]{2,1,0:T(8,128)(2,1)} %get-tuple-element.211.qt, ...), custom_call_target="tpu_custom_call" | custom-call | flops 18936666112 | bytes 60762000 | tf_op jit(solution)/shard_map/pallas_call | solution.py:107
  190.8 0.8 copy-done.40
  191.6 17.1 %shard_map.518 = (bf16[4,784,128]{2,1,0:T(8,128)(2,1)}, bf16[4,128,784]{2,1,0:T(8,128)(2,1)}, bf16[2,912,384]{2,1,0:T(8,128)(2,1)}, bf16[2,912,384]{2,1,0:T(8,12...) custom-call(s32[2]{0:T(128)} %pad_add_fusion.spot, f32[784,384]{1,0:T(8,128)} %get-tuple-element.229.dx_own, ...), custom_call_target="tpu_custom_call" | custom-call | flops 19549999104 | bytes 62730000 | tf_op jit(solution)/shard_map/pallas_call | solution.py:107
  209.0 1.2 copy-done.37
  210.3 1.8 collective-permute-start.17
  212.1 1.5 collective-permute-start.16
  213.6 19.9 %shard_map.519 = (f32[2,784,128]{2,1,0:T(8,128)}, f32[2,2,96,192]{3,2,1,0:T(8,128)}, f32[2,8,128]{2,1,0:T(8,128)}, f32[192,3136]{1,0:T(8,128)}) custom-call(bf16[4,784,128]{2,1,0:T(8,128)(2,1)} %get-tuple-element.206.qb, bf16[4,128,784]{2,1,0:T(8,128)(2,1)} %get-tuple-element.207.qt, bf16[4,784,128]{2,1,0:T(8,128)(2,1)} %get-tuple-element.240.do, ...), custom_call_target="tpu_custom_call" | custom-call | flops 1150000000 | bytes 3690000 | tf_op jit(solution)/shard_map/pallas_call | solution.py:107
  233.6 0.7 add_convert_fusion.9
  235.4 2.7 collective-permute-start.19
  238.6 19.7 %shard_map.520 = (f32[2,784,128]{2,1,0:T(8,128)}, f32[2,2,96,192]{3,2,1,0:T(8,128)}, f32[2,8,128]{2,1,0:T(8,128)}, bf16[192,3136]{1,0:T(8,128)(2,1)}) custom-call(bf16[4,784,128]{2,1,0:T(8,128)(2,1)} %get-tuple-element.206.qb, bf16[4,128,784]{2,1,0:T(8,128)(2,1)} %get-tuple-element.207.qt, bf16[4,784,128]{2,1,0:T(8,128)(2,1)} %get-tuple-element.240.do, ...), custom_call_target="tpu_custom_call" | custom-call | flops 1150000000 | bytes 3690000 | tf_op jit(solution)/shard_map/pallas_call | solution.py:107
  258.3 1.6 collective-permute-start.18
  259.9 7.1 %collective-permute-done.19 = bf16[864,384]{1,0:T(8,128)(2,1)S(1)} collective-permute-done((bf16[864,384]{1,0:T(8,128)(2,1)S(1)}, bf16[864,384]{1,0:T(8,128)(2,1)S(1)}, u32[]{:S(2)}, u32[]{:S(2)}) %collective-permute-start.19) | collective-permute-done | bytes 663584 | tf_op jit(solution)/shard_map/ppermute | solution.py:876
  267.2 1.0 add_convert_fusion
  268.3 1.5 collective-permute-start.21
  269.8 22.1 %shard_map.521 = (bf16[1,3,96,192]{3,2,1,0:T(8,128)(2,1)}, bf16[1,3,96,192]{3,2,1,0:T(8,128)(2,1)}, f32[8,384]{1,0:T(8,128)}, f32[192,3136]{1,0:T(8,128)}, f32[192,784]{1,0:T(8,128)}) custom-call(s32[2]{0:T(128)} %pad_add_fusion.spot, bf16[4,784,128]{2,1,0:T(8,128)(2,1)} %get-tuple-element.206.qb, bf16[4,128,784]{2,1,0:T(8,128)(2,1)} %get-tuple-element.207.qt, ...), custom_call_target="tpu_custom_call" | custom-call | flops 23000000512 | bytes 73800000 | tf_op jit(solution)/shard_map/pallas_call | solution.py:107
  293.2 29.6 %shard_map.522 = (bf16[1,3,96,192]{3,2,1,0:T(8,128)(2,1)}, bf16[1,3,96,192]{3,2,1,0:T(8,128)(2,1)}, f32[16,384]{1,0:T(8,128)}, f32[3136,192]{1,0:T(8,128)}) custom-call(s32[2]{0:T(128)} %pad_add_fusion.spot, bf16[4,784,128]{2,1,0:T(8,128)(2,1)} %get-tuple-element.206.qb, bf16[4,128,784]{2,1,0:T(8,128)(2,1)} %get-tuple-element.207.qt, ...), custom_call_target="tpu_custom_call" | custom-call | flops 345000000 | bytes 1107000 | tf_op jit(solution)/shard_map/pallas_call | solution.py:107
  324.9 1.4 collective-permute-start.23
  326.3 3.5 copy.89
  329.8 2.1 collective-permute-done.23
  332.1 15.9 %all-reduce.5.cloned.1.call-done = (bf16[912,384]{1,0:T(8,128)(2,1)}, bf16[3,96,384]{2,1,0:T(8,128)(2,1)}) async-done(((bf16[912,384]{1,0:T(8,128)(2,1)}, bf16[3,96,384]{2,1,0:T(8,128)(2,1)}), (bf16[912,384]{1,0:T(8,128)(2,1)}, bf16[3,96,384]{2,1,0:T(8,128)(2,1)})) %all-reduce.5.cloned.1.call-update) | async-done | bytes 921616 | tf_op jit(solution)/shard_map/psum | solution.py:1084
  348.0 1.0 collective-permute-start.32
  349.0 1.8 collective-permute-start.25
  350.8 0.8 slice_bitcast_fusion.1
  352.1 2.6 collective-permute-done.25
  354.7 1.9 collective-permute-start.26
  356.7 1.0 collective-permute-start.33
  357.7 1.6 collective-permute-done.26
  359.9 1.6 shard_map.523
  361.5 2.8 collective-permute-done.33
  365.3 2.7 shard_map.526
  368.0 2.3 copy.91
  370.5 0.8 copy-done.38
  371.3 3.1 shard_map.527
  374.4 1.4 collective-permute-start.31
  376.5 2.2 shard_map.525
  378.7 2.1 copy.90
  381.4 3.2 shard_map.524
  (200 shorter events, 14.4 us)
Async XLA Ops:
  7.2 6.2 %copy-start = (s32[1,1568]{1,0:T(1,128)S(1)}, s32[1,1568]{1,0:T(1,128)}, u32[]{:S(2)}) copy-start(s32[1,1568]{1,0:T(1,128)} %param.34) | copy-start | bytes 18820
  7.2 8.3 %copy-start.10 = (bf16[768,384]{1,0:T(8,128)(2,1)S(1)}, bf16[768,384]{1,0:T(8,128)(2,1)}, u32[]{:S(2)}) copy-start(bf16[768,384]{1,0:T(8,128)(2,1)} %param.59) | copy-start | bytes 1769476
  7.2 8.7 %copy-start.12 = (bf16[384,768]{1,0:T(8,128)(2,1)S(1)}, bf16[384,768]{1,0:T(8,128)(2,1)}, u32[]{:S(2)}) copy-start(bf16[384,768]{1,0:T(8,128)(2,1)} %up_own.4) | copy-start | bytes 1769476
  7.2 340.7 %all-reduce.5.cloned.1.call-start = ((), (), s32[]{:S(2)}) async-start(), calls=%async_computation | async-start | bytes 1843200 | tf_op jit(solution)/shard_map/psum | solution.py:1084
  10.3 6.5 %copy-start.22 = (f32[3,768]{1,0:T(4,128)}, f32[3,768]{1,0:T(4,128)S(1)}, u32[]{:S(2)}) copy-start(f32[3,768]{1,0:T(4,128)S(1)} %pad_maximum_fusion.1.pack_own) | copy-start | bytes 27652
  10.3 12.1 %collective-permute-start.1 = (f32[3,768]{1,0:T(4,128)S(1)}, f32[3,768]{1,0:T(4,128)S(1)}, u32[]{:S(2)}, u32[]{:S(2)}) collective-permute-start(f32[3,768]{1,0:T(4,128)S(1)} %pad_maximum_fusion.1.pack_own), channel_id=1, source_target_pairs={{0,1},{1,0},{2,3},{3,2},{4,5},{5,4},{6,7},{7,6},{8,9},{9,8},{10,11... | collective-permute-start | bytes 27656 | tf_op jit(solution)/shard_map/ppermute | solution.py:860
  13.4 9.0 %collective-permute-start = (bf16[3,192,192]{2,1,0:T(8,128)(2,1)}, bf16[3,192,192]{2,1,0:T(8,128)(2,1)}, u32[]{:S(2)}, u32[]{:S(2)}) collective-permute-start(bf16[3,192,192]{2,1,0:T(8,128)(2,1)} %bitcast.44), channel_id=1, source_target_pairs={{0,1},{1,0},{2,3},{3,2},{4,5},{5,4},{6,7},{7,6},{8,9},{9,8},{10,11... | collective-permute-start | bytes 663560 | tf_op jit(solution)/shard_map/ppermute | solution.py:860
  15.6 2.7 copy-start.36
  15.6 2.7 copy-start.11
  15.9 3.6 copy-start.3
  15.9 3.6 copy-start.14
  16.8 2.9 copy-start.7
  19.7 70.9 %copy-start.4 = (bf16[384,3,192]{2,0,1:T(8,128)(2,1)}, bf16[384,3,192]{2,0,1:T(8,128)(2,1)S(1)}, u32[]{:S(2)}) copy-start(bf16[384,3,192]{2,0,1:T(8,128)(2,1)S(1)} %copy.78) | copy-start | bytes 1327108
  21.1 3.3 copy-start.2
  24.3 33.5 %collective-permute-start.2 = (bf16[3136,192]{0,1:T(8,128)(2,1)}, bf16[3136,192]{0,1:T(8,128)(2,1)S(1)}, u32[]{:S(2)}, u32[]{:S(2)}) collective-permute-start(bf16[3136,192]{0,1:T(8,128)(2,1)} %copy.80), channel_id=1, source_target_pairs={{0,1},{1,0},{2,3},{3,2},{4,5},{5,4},{6,7},{7,6},{8,9},{9,8},{10,11... | collective-permute-start | bytes 3612680 | tf_op jit(solution)/shard_map/ppermute | solution.py:860
  55.6 35.4 %collective-permute-start.5 = (bf16[192,384]{1,0:T(8,128)(2,1)}, bf16[192,384]{1,0:T(8,128)(2,1)}, u32[]{:S(2)}, u32[]{:S(2)}) collective-permute-start(bf16[192,384]{1,0:T(8,128)(2,1)} %wo_own.5), channel_id=1, source_target_pairs={{0,1},{1,0},{2,3},{3,2},{4,5},{5,4},{6,7},{7,6},{8,9},{9,8},{10,11... | collective-permute-start | bytes 442376 | tf_op jit(solution)/shard_map/ppermute | solution.py:860
  55.8 35.3 %collective-permute-start.6 = (bf16[384,768]{1,0:T(8,128)(2,1)}, bf16[384,768]{1,0:T(8,128)(2,1)S(1)}, u32[]{:S(2)}, u32[]{:S(2)}) collective-permute-start(bf16[384,768]{1,0:T(8,128)(2,1)} %up_own.5), channel_id=1, source_target_pairs={{0,1},{1,0},{2,3},{3,2},{4,5},{5,4},{6,7},{7,6},{8,9},{9,8},{10,11... | collective-permute-start | bytes 1769480 | tf_op jit(solution)/shard_map/ppermute | solution.py:860
  57.7 33.4 %collective-permute-start.7 = (bf16[384,768]{1,0:T(8,128)(2,1)}, bf16[384,768]{1,0:T(8,128)(2,1)}, u32[]{:S(2)}, u32[]{:S(2)}) collective-permute-start(bf16[384,768]{1,0:T(8,128)(2,1)} %bitcast.7.down_own), channel_id=1, source_target_pairs={{0,1},{1,0},{2,3},{3,2},{4,5},{5,4},{6,7},{7,6},{8,9},{9,8},{10,11... | collective-permute-start | bytes 1769480 | tf_op jit(solution)/shard_map/ppermute | solution.py:860
  59.5 29.1 %copy-start.45 = (bf16[192,384]{1,0:T(8,128)(2,1)S(1)}, bf16[192,384]{1,0:T(8,128)(2,1)}, u32[]{:S(2)}) copy-start(bf16[192,384]{1,0:T(8,128)(2,1)} %wo_own.4) | copy-start | bytes 442372
  88.6 30.8 %collective-permute-start.9 = (bf16[192,384]{1,0:T(8,128)(2,1)S(1)}, bf16[192,384]{1,0:T(8,128)(2,1)S(1)}, u32[]{:S(2)}, u32[]{:S(2)}) collective-permute-start(bf16[192,384]{1,0:T(8,128)(2,1)S(1)} %copy-done.45), channel_id=1, source_target_pairs={{0,1},{1,0},{2,3},{3,2},{4,5},{5,4},{6,7},{7,6},{8,9},{9,8},{10,11... | collective-permute-start | bytes 442376 | tf_op jit(solution)/shard_map/ppermute | solution.py:860
  90.9 13.9 %collective-permute-start.3 = (bf16[3,384,192]{1,2,0:T(8,128)(2,1)S(1)}, bf16[3,384,192]{1,2,0:T(8,128)(2,1)S(1)}, u32[]{:S(2)}, u32[]{:S(2)}) collective-permute-start(bf16[3,384,192]{1,2,0:T(8,128)(2,1)S(1)} %copy.87), channel_id=1, source_target_pairs={{0,1},{1,0},{2,3},{3,2},{4,5},{5,4},{6,7},{7,6},{8,9},{9,8},{10,11... | collective-permute-start | bytes 1327112 | tf_op jit(solution)/shard_map/ppermute | solution.py:860
  91.9 14.0 %copy-start.13 = (bf16[384,768]{1,0:T(8,128)(2,1)S(1)}, bf16[384,768]{1,0:T(8,128)(2,1)}, u32[]{:S(2)}) copy-start(bf16[384,768]{1,0:T(8,128)(2,1)} %broadcast_select_fusion) | copy-start | bytes 1769476
  102.9 16.7 %collective-permute-start.8 = (bf16[784,384]{1,0:T(8,128)(2,1)}, bf16[784,384]{1,0:T(8,128)(2,1)S(1)}, u32[]{:S(2)}, u32[]{:S(2)}) collective-permute-start(bf16[784,384]{1,0:T(8,128)(2,1)} %get-tuple-element.190.x), channel_id=1, source_target_pairs={{0,1},{1,0},{2,3},{3,2},{4,5},{5,4},{6,7},{7,6},{8,9},{9,8},{10,11... | collective-permute-start | bytes 1806344 | tf_op jit(solution)/shard_map/ppermute | solution.py:860
  105.9 28.7 %collective-permute-start.4 = (bf16[384,768]{1,0:T(8,128)(2,1)S(1)}, bf16[384,768]{1,0:T(8,128)(2,1)S(1)}, u32[]{:S(2)}, u32[]{:S(2)}) collective-permute-start(bf16[384,768]{1,0:T(8,128)(2,1)S(1)} %copy-done.13), channel_id=1, source_target_pairs={{0,1},{1,0},{2,3},{3,2},{4,5},{5,4},{6,7},{7,6},{8,9},{9,8},{10,11... | collective-permute-start | bytes 1769480 | tf_op jit(solution)/shard_map/ppermute | solution.py:860
  119.5 15.1 %copy-start.46 = (bf16[192,384]{1,0:T(8,128)(2,1)}, bf16[192,384]{1,0:T(8,128)(2,1)S(1)}, u32[]{:S(2)}) copy-start(bf16[192,384]{1,0:T(8,128)(2,1)S(1)} %collective-permute-done.9.wo_far) | copy-start | bytes 442372
  134.6 2.1 collective-permute-start.10
  156.3 15.9 %collective-permute-start.11 = (bf16[2,864,384]{2,1,0:T(8,128)(2,1)}, bf16[2,864,384]{2,1,0:T(8,128)(2,1)S(1)}, u32[]{:S(2)}, u32[]{:S(2)}) collective-permute-start(bf16[2,864,384]{2,1,0:T(8,128)(2,1)} %get-tuple-element.209), channel_id=1, source_target_pairs={{0,2},{2,0},{1,3},{3,1},{4,6},{6,4},{5,7},{7,5},{8,10},{10,8},{9,1... | collective-permute-start | bytes 3981320 | tf_op jit(solution)/shard_map/ppermute | solution.py:864
  156.4 15.7 %copy-start.6 = (bf16[2,864,384]{2,1,0:T(8,128)(2,1)S(1)}, bf16[2,864,384]{2,1,0:T(8,128)(2,1)}, u32[]{:S(2)}) copy-start(bf16[2,864,384]{2,1,0:T(8,128)(2,1)} %get-tuple-element.208) | copy-start | bytes 3981316
  170.1 20.6 %collective-permute-start.14 = (bf16[784,384]{1,0:T(8,128)(2,1)}, bf16[784,384]{1,0:T(8,128)(2,1)S(1)}, u32[]{:S(2)}, u32[]{:S(2)}) collective-permute-start(bf16[784,384]{1,0:T(8,128)(2,1)} %get-tuple-element.230), channel_id=1, source_target_pairs={{0,1},{1,0},{2,3},{3,2},{4,5},{5,4},{6,7},{7,6},{8,9},{9,8},{10,11... | collective-permute-start | bytes 1806344 | tf_op jit(solution)/shard_map/ppermute | solution.py:860
  190.3 18.4 %collective-permute-start.13 = (bf16[2,3,96,384]{3,2,1,0:T(8,128)(2,1)}, bf16[2,3,96,384]{3,2,1,0:T(8,128)(2,1)S(1)}, u32[]{:S(2)}, u32[]{:S(2)}) collective-permute-start(bf16[2,3,96,384]{3,2,1,0:T(8,128)(2,1)} %get-tuple-element.228), channel_id=1, source_target_pairs={{0,2},{2,0},{1,3},{3,1},{4,6},{6,4},{5,7},{7,5},{8,10},{10,8},{9,1... | collective-permute-start | bytes 1327112 | tf_op jit(solution)/shard_map/ppermute | solution.py:864
  190.5 18.4 %collective-permute-start.12 = (bf16[864,384]{1,0:T(8,128)(2,1)S(1)}, bf16[864,384]{1,0:T(8,128)(2,1)S(1)}, u32[]{:S(2)}, u32[]{:S(2)}) collective-permute-start(bf16[864,384]{1,0:T(8,128)(2,1)S(1)} %get-tuple-element.226), channel_id=1, source_target_pairs={{0,1},{1,0},{2,3},{3,2},{4,5},{5,4},{6,7},{7,6},{8,9},{9,8},{10,11... | collective-permute-start | bytes 1990664 | tf_op jit(solution)/shard_map/ppermute | solution.py:860
  191.6 17.1 %copy-start.15 = (bf16[2,3,96,384]{3,2,1,0:T(8,128)(2,1)S(1)}, bf16[2,3,96,384]{3,2,1,0:T(8,128)(2,1)}, u32[]{:S(2)}) copy-start(bf16[2,3,96,384]{3,2,1,0:T(8,128)(2,1)} %get-tuple-element.227) | copy-start | bytes 1327108
  210.2 24.4 %collective-permute-start.15 = (bf16[2,912,384]{2,1,0:T(8,128)(2,1)S(1)}, bf16[2,912,384]{2,1,0:T(8,128)(2,1)S(1)}, u32[]{:S(2)}, u32[]{:S(2)}) collective-permute-start(bf16[2,912,384]{2,1,0:T(8,128)(2,1)S(1)} %copy-done.37), channel_id=1, source_target_pairs={{0,2},{2,0},{1,3},{3,1},{4,6},{6,4},{5,7},{7,5},{8,10},{10,8},{9,1... | collective-permute-start | bytes 4202504 | tf_op jit(solution)/shard_map/ppermute | solution.py:864
  210.3 24.0 %collective-permute-start.17 = (bf16[864,384]{1,0:T(8,128)(2,1)S(1)}, bf16[864,384]{1,0:T(8,128)(2,1)S(1)}, u32[]{:S(2)}, u32[]{:S(2)}) collective-permute-start(bf16[864,384]{1,0:T(8,128)(2,1)S(1)} %add_convert_fusion.6), channel_id=1, source_target_pairs={{0,8},{4,12},{8,0},{12,4},{16,24},{20,28},{24,16},{28,20},{1,9},{5... | collective-permute-start | bytes 1990664 | tf_op jit(solution)/shard_map/ppermute | solution.py:876
  212.1 21.5 %collective-permute-start.16 = (bf16[3,96,384]{2,1,0:T(8,128)(2,1)S(1)}, bf16[3,96,384]{2,1,0:T(8,128)(2,1)S(1)}, u32[]{:S(2)}, u32[]{:S(2)}) collective-permute-start(bf16[3,96,384]{2,1,0:T(8,128)(2,1)S(1)} %get-tuple-element.252), channel_id=1, source_target_pairs={{0,1},{1,0},{2,3},{3,2},{4,5},{5,4},{6,7},{7,6},{8,9},{9,8},{10,11... | collective-permute-start | bytes 663560 | tf_op jit(solution)/shard_map/ppermute | solution.py:860
  235.0 3.5 copy-start.19
  235.0 3.6 copy-start.20
  235.0 3.6 copy-start.21
  235.4 31.7 %collective-permute-start.19 = (bf16[864,384]{1,0:T(8,128)(2,1)S(1)}, bf16[864,384]{1,0:T(8,128)(2,1)S(1)}, u32[]{:S(2)}, u32[]{:S(2)}) collective-permute-start(bf16[864,384]{1,0:T(8,128)(2,1)S(1)} %add_convert_fusion.5), channel_id=1, source_target_pairs={{0,16},{4,20},{8,24},{12,28},{16,0},{20,4},{24,8},{28,12},{1,17},{... | collective-permute-start | bytes 1990664 | tf_op jit(solution)/shard_map/ppermute | solution.py:876
  238.0 29.2 %collective-permute-start.20 = (bf16[912,384]{1,0:T(8,128)(2,1)S(1)}, bf16[912,384]{1,0:T(8,128)(2,1)S(1)}, u32[]{:S(2)}, u32[]{:S(2)}) collective-permute-start(bf16[912,384]{1,0:T(8,128)(2,1)S(1)} %get-tuple-element.259), channel_id=1, source_target_pairs={{0,1},{1,0},{2,3},{3,2},{4,5},{5,4},{6,7},{7,6},{8,9},{9,8},{10,11... | collective-permute-start | bytes 2101256 | tf_op jit(solution)/shard_map/ppermute | solution.py:860
  258.3 33.8 %collective-permute-start.18 = (bf16[192,3136]{1,0:T(8,128)(2,1)}, bf16[192,3136]{1,0:T(8,128)(2,1)S(1)}, u32[]{:S(2)}, u32[]{:S(2)}) collective-permute-start(bf16[192,3136]{1,0:T(8,128)(2,1)} %get-tuple-element.256), channel_id=1, source_target_pairs={{0,1},{1,0},{2,3},{3,2},{4,5},{5,4},{6,7},{7,6},{8,9},{9,8},{10,11... | collective-permute-start | bytes 3612680 | tf_op jit(solution)/shard_map/ppermute | solution.py:860
  268.3 23.6 %collective-permute-start.21 = (bf16[864,384]{1,0:T(8,128)(2,1)S(1)}, bf16[864,384]{1,0:T(8,128)(2,1)S(1)}, u32[]{:S(2)}, u32[]{:S(2)}) collective-permute-start(bf16[864,384]{1,0:T(8,128)(2,1)S(1)} %add_convert_fusion.4), channel_id=1, source_target_pairs={{0,4},{4,0},{8,12},{12,8},{16,20},{20,16},{24,28},{28,24},{1,5},{5... | collective-permute-start | bytes 1990664 | tf_op jit(solution)/shard_map/ppermute | solution.py:876
  292.1 37.7 %copy-start.9 = (bf16[864,384]{1,0:T(8,128)(2,1)}, bf16[864,384]{1,0:T(8,128)(2,1)S(1)}, u32[]{:S(2)}) copy-start(bf16[864,384]{1,0:T(8,128)(2,1)S(1)} %add_convert_fusion.3.mine) | copy-start | bytes 1990660
  292.8 31.3 %collective-permute-start.28 = (bf16[1,3,96,192]{3,2,1,0:T(8,128)(2,1)S(1)}, bf16[1,3,96,192]{3,2,1,0:T(8,128)(2,1)S(1)}, u32[]{:S(2)}, u32[]{:S(2)}) collective-permute-start(bf16[1,3,96,192]{3,2,1,0:T(8,128)(2,1)S(1)} %copy-done.47), channel_id=1, source_target_pairs={{0,2},{2,0},{1,3},{3,1},{4,6},{6,4},{5,7},{7,5},{8,10},{10,8},{9,1... | collective-permute-start | bytes 331784 | tf_op jit(solution)/shard_map/ppermute | solution.py:864
  293.2 30.9 %copy-start.16 = (bf16[1,3,96,192]{3,2,1,0:T(8,128)(2,1)S(1)}, bf16[1,3,96,192]{3,2,1,0:T(8,128)(2,1)}, u32[]{:S(2)}) copy-start(bf16[1,3,96,192]{3,2,1,0:T(8,128)(2,1)} %get-tuple-element.290) | copy-start | bytes 331780
  323.6 1.3 collective-permute-start.22
  323.7 8.3 %collective-permute-start.27 = (bf16[1,3,96,192]{3,2,1,0:T(8,128)(2,1)}, bf16[1,3,96,192]{3,2,1,0:T(8,128)(2,1)S(1)}, u32[]{:S(2)}, u32[]{:S(2)}) collective-permute-start(bf16[1,3,96,192]{3,2,1,0:T(8,128)(2,1)} %get-tuple-element.289), channel_id=1, source_target_pairs={{0,2},{2,0},{1,3},{3,1},{4,6},{6,4},{5,7},{7,5},{8,10},{10,8},{9,1... | collective-permute-start | bytes 331784 | tf_op jit(solution)/shard_map/ppermute | solution.py:864
  324.1 7.9 %collective-permute-start.29 = (bf16[3,96,192]{2,1,0:T(8,128)(2,1)S(1)}, bf16[3,96,192]{2,1,0:T(8,128)(2,1)S(1)}, u32[]{:S(2)}, u32[]{:S(2)}) collective-permute-start(bf16[3,96,192]{2,1,0:T(8,128)(2,1)S(1)} %fusion.35), channel_id=1, source_target_pairs={{0,1},{1,0},{2,3},{3,2},{4,5},{5,4},{6,7},{7,6},{8,9},{9,8},{10,11... | collective-permute-start | bytes 331784 | tf_op jit(solution)/shard_map/ppermute | solution.py:860
  324.9 7.0 %collective-permute-start.23 = (f32[56,384]{1,0:T(8,128)S(1)}, f32[56,384]{1,0:T(8,128)S(1)}, u32[]{:S(2)}, u32[]{:S(2)}) collective-permute-start(f32[56,384]{1,0:T(8,128)S(1)} %add.209), channel_id=1, source_target_pairs={{0,1},{1,0},{2,3},{3,2},{4,5},{5,4},{6,7},{7,6},{8,9},{9,8},{10,11... | collective-permute-start | bytes 258056 | tf_op jit(solution)/shard_map/ppermute | solution.py:876
  326.3 5.7 %copy-start.18 = (bf16[1,3,96,192]{3,2,1,0:T(8,128)(2,1)S(1)}, bf16[1,3,96,192]{3,2,1,0:T(8,128)(2,1)}, u32[]{:S(2)}) copy-start(bf16[1,3,96,192]{3,2,1,0:T(8,128)(2,1)} %get-tuple-element.288) | copy-start | bytes 331780
  329.8 40.7 %collective-permute-start.37 = (bf16[864,384]{1,0:T(8,128)(2,1)S(1)}, bf16[864,384]{1,0:T(8,128)(2,1)S(1)}, u32[]{:S(2)}, u32[]{:S(2)}) collective-permute-start(bf16[864,384]{1,0:T(8,128)(2,1)S(1)} %add_convert_fusion.3.mine), channel_id=1, source_target_pairs={{0,2},{2,0},{1,3},{3,1},{4,6},{6,4},{5,7},{7,5},{8,10},{10,8},{9,1... | collective-permute-start | bytes 1990664 | tf_op jit(solution)/shard_map/ppermute | solution.py:864
  331.9 17.1 %collective-permute-start.24 = (f32[56,384]{1,0:T(8,128)S(1)}, f32[56,384]{1,0:T(8,128)S(1)}, u32[]{:S(2)}, u32[]{:S(2)}) collective-permute-start(f32[56,384]{1,0:T(8,128)S(1)} %add.210), channel_id=1, source_target_pairs={{0,8},{4,12},{8,0},{12,4},{16,24},{20,28},{24,16},{28,20},{1,9},{5... | collective-permute-start | bytes 258056 | tf_op jit(solution)/shard_map/ppermute | solution.py:876
  348.0 8.6 %collective-permute-start.32 = (bf16[3,96,192]{2,1,0:T(8,128)(2,1)S(1)}, bf16[3,96,192]{2,1,0:T(8,128)(2,1)S(1)}, u32[]{:S(2)}, u32[]{:S(2)}) collective-permute-start(bf16[3,96,192]{2,1,0:T(8,128)(2,1)S(1)} %fusion.31), channel_id=1, source_target_pairs={{0,8},{4,12},{8,0},{12,4},{16,24},{20,28},{24,16},{28,20},{1,9},{5... | collective-permute-start | bytes 331784 | tf_op jit(solution)/shard_map/ppermute | solution.py:876
  349.0 5.7 %collective-permute-start.25 = (f32[56,384]{1,0:T(8,128)S(1)}, f32[56,384]{1,0:T(8,128)S(1)}, u32[]{:S(2)}, u32[]{:S(2)}) collective-permute-start(f32[56,384]{1,0:T(8,128)S(1)} %add.211), channel_id=1, source_target_pairs={{0,16},{4,20},{8,24},{12,28},{16,0},{20,4},{24,8},{28,12},{1,17},{... | collective-permute-start | bytes 258056 | tf_op jit(solution)/shard_map/ppermute | solution.py:876
  351.6 22.8 %collective-permute-start.30 = (bf16[912,384]{1,0:T(8,128)(2,1)}, bf16[912,384]{1,0:T(8,128)(2,1)S(1)}, u32[]{:S(2)}, u32[]{:S(2)}) collective-permute-start(bf16[912,384]{1,0:T(8,128)(2,1)} %get-tuple-element.292.mine), channel_id=1, source_target_pairs={{0,2},{2,0},{1,3},{3,1},{4,6},{6,4},{5,7},{7,5},{8,10},{10,8},{9,1... | collective-permute-start | bytes 2101256 | tf_op jit(solution)/shard_map/ppermute | solution.py:864
  351.6 13.1 %collective-permute-start.36 = (bf16[3,96,384]{2,1,0:T(8,128)(2,1)}, bf16[3,96,384]{2,1,0:T(8,128)(2,1)S(1)}, u32[]{:S(2)}, u32[]{:S(2)}) collective-permute-start(bf16[3,96,384]{2,1,0:T(8,128)(2,1)} %get-tuple-element.307.mine), channel_id=1, source_target_pairs={{0,2},{2,0},{1,3},{3,1},{4,6},{6,4},{5,7},{7,5},{8,10},{10,8},{9,1... | collective-permute-start | bytes 663560 | tf_op jit(solution)/shard_map/ppermute | solution.py:864
  354.7 4.6 %collective-permute-start.26 = (f32[56,384]{1,0:T(8,128)S(1)}, f32[56,384]{1,0:T(8,128)S(1)}, u32[]{:S(2)}, u32[]{:S(2)}) collective-permute-start(f32[56,384]{1,0:T(8,128)S(1)} %add.212), channel_id=1, source_target_pairs={{0,4},{4,0},{8,12},{12,8},{16,20},{20,16},{24,28},{28,24},{1,5},{5... | collective-permute-start | bytes 258056 | tf_op jit(solution)/shard_map/ppermute | solution.py:876
  356.7 7.6 %collective-permute-start.33 = (bf16[3,96,192]{2,1,0:T(8,128)(2,1)S(1)}, bf16[3,96,192]{2,1,0:T(8,128)(2,1)S(1)}, u32[]{:S(2)}, u32[]{:S(2)}) collective-permute-start(bf16[3,96,192]{2,1,0:T(8,128)(2,1)S(1)} %add_convert_fusion.14), channel_id=1, source_target_pairs={{0,16},{4,20},{8,24},{12,28},{16,0},{20,4},{24,8},{28,12},{1,17},{... | collective-permute-start | bytes 331784 | tf_op jit(solution)/shard_map/ppermute | solution.py:876
  364.3 6.0 %collective-permute-start.34 = (bf16[3,96,192]{2,1,0:T(8,128)(2,1)S(1)}, bf16[3,96,192]{2,1,0:T(8,128)(2,1)S(1)}, u32[]{:S(2)}, u32[]{:S(2)}) collective-permute-start(bf16[3,96,192]{2,1,0:T(8,128)(2,1)S(1)} %add_convert_fusion.13), channel_id=1, source_target_pairs={{0,4},{4,0},{8,12},{12,8},{16,20},{20,16},{24,28},{28,24},{1,5},{5... | collective-permute-start | bytes 331784 | tf_op jit(solution)/shard_map/ppermute | solution.py:876
  370.4 4.0 %copy-start.17 = (bf16[3,96,192]{2,1,0:T(8,128)(2,1)}, bf16[3,96,192]{2,1,0:T(8,128)(2,1)S(1)}, u32[]{:S(2)}) copy-start(bf16[3,96,192]{2,1,0:T(8,128)(2,1)S(1)} %add_convert_fusion.12.mine) | copy-start | bytes 331780
  370.4 5.5 %collective-permute-start.35 = (bf16[3,96,192]{2,1,0:T(8,128)(2,1)S(1)}, bf16[3,96,192]{2,1,0:T(8,128)(2,1)S(1)}, u32[]{:S(2)}, u32[]{:S(2)}) collective-permute-start(bf16[3,96,192]{2,1,0:T(8,128)(2,1)S(1)} %add_convert_fusion.12.mine), channel_id=1, source_target_pairs={{0,2},{2,0},{1,3},{3,1},{4,6},{6,4},{5,7},{7,5},{8,10},{10,8},{9,1... | collective-permute-start | bytes 331784 | tf_op jit(solution)/shard_map/ppermute | solution.py:864
  374.4 4.3 %copy-start.34 = (bf16[912,384]{1,0:T(8,128)(2,1)}, bf16[912,384]{1,0:T(8,128)(2,1)S(1)}, u32[]{:S(2)}) copy-start(bf16[912,384]{1,0:T(8,128)(2,1)S(1)} %collective-permute-done.30.other) | copy-start | bytes 2101252
  374.4 6.4 %collective-permute-start.31 = (bf16[2,48,384]{2,1,0:T(8,128)(2,1)S(1)}, bf16[2,48,384]{2,1,0:T(8,128)(2,1)S(1)}, u32[]{:S(2)}, u32[]{:S(2)}) collective-permute-start(bf16[2,48,384]{2,1,0:T(8,128)(2,1)S(1)} %pad_maximum_fusion), channel_id=1, source_target_pairs={{0,1},{1,0},{2,3},{3,2},{4,5},{5,4},{6,7},{7,6},{8,9},{9,8},{10,11... | collective-permute-start | bytes 221192 | tf_op jit(solution)/shard_map/ppermute | solution.py:860
  381.4 3.2 copy-start.1
  (26 other events, 46.6 us)
Sparse Core Ops, SparseCore 0:
  269.9 77.9 all-reduce.4
